TPU v7x, 512 devices: a whole 4x4x16 slice. The times are simulated.
512 devices in a mesh: wide: 32 (over z, core), narrow: 16 (over x, y).
Axes of the slice: x: 4, y: 4, z: 16, core: 2. Of those that a mesh axis runs over, the one named last changes fastest.
Arguments:
- positions: float32 [16384, 3, 256], P(('wide', 'narrow')), may hold values from -1 to 1
- moments: float32 [16384, 3, 256], P(('wide', 'narrow')), may hold values from -6 to 6
- counts: int32 [16384], P(('wide', 'narrow')), may hold values from 1 to 256
- dest: int32 [16384], P(('wide', 'narrow')), may hold values from 0 to 15, as said below
Outputs:
- leaf_multipoles: float32 [65536, 286], P(('wide', 'narrow'))
- box_multipoles: float32 [13312, 286], P(('wide', 'narrow'))
Inputs may be any that keep to these rules, and one draw needn't show every extreme that they name: `dest`: each device sends at most 8 of its blocks to one owner, and in every group one owner receives exactly 8 blocks from every device of the group.
All inputs are finite; a program needn't handle non-finite values.
Results may differ from a plain program's by a relative error of at most 0.0003.
Values sent between devices are 32-bit elements; how exact they have to be, the bound alone decides.
No kernel may reach another device: no remote copies, remote signals or barrier semaphores. Data moves between devices by JAX's collectives and lax.ppermute only.
A program may use at most 64 MiB of HBM per device.

v0:
```python
import math

import jax
import jax.numpy as jnp
import numpy as np
from jax import lax
from jax.sharding import PartitionSpec as P

P_SIZE = 10
LEVELS = 5


def exponent_list(order):
    triples = []
    for degree in range(order + 1):
        for power_x in range(degree, -1, -1):
            for power_y in range(degree - power_x, -1, -1):
                triples.append((power_x, power_y, degree - power_x - power_y))
    return triples


def source_tables(order):
    triples = exponent_list(order)
    pick_index = np.zeros((3, len(triples)), np.int32)
    weights = np.zeros((3, len(triples)), np.float32)
    for column, triple in enumerate(triples):
        for axis_id in range(3):
            if triple[axis_id] > 0:
                lowered = list(triple)
                lowered[axis_id] -= 1
                pick_index[axis_id, column] = (
                    (axis_id * order + lowered[2]) * order + lowered[0]
                ) * order + lowered[1]
                weights[axis_id, column] = triple[axis_id] / 16.0
    return (pick_index, weights)


def shift_table(order):
    triples = exponent_list(order)
    term_count = len(triples)
    table = np.zeros((8 * term_count, term_count), np.float32)
    for octant in range(8):
        sign_list = [2 * (octant >> axis_id & 1) - 1 for axis_id in range(3)]
        for column, target_exp in enumerate(triples):
            halving = 0.5 ** sum(target_exp)
            for source_row, source_exp in enumerate(triples):
                if all((source_exp[axis_id] <= target_exp[axis_id] for axis_id in range(3))):
                    entry_value = halving
                    for axis_id in range(3):
                        entry_value *= math.comb(
                            target_exp[axis_id], source_exp[axis_id]
                        ) * sign_list[axis_id] ** (target_exp[axis_id] - source_exp[axis_id])
                    table[octant * term_count + source_row, column] = entry_value
    return table


def block_moments(positions, moments, counts, order):
    total_rows = positions.shape[0]
    per_block = positions.shape[2]
    pick_index, weights = source_tables(order)
    weight_rows = jnp.asarray(weights, jnp.float32)
    batch_rows = math.gcd(total_rows, 64)

    def one_batch(batch_in):
        places, dipoles, live_counts = batch_in
        living = (jnp.arange(per_block)[None, :] < live_counts[:, None]).astype(jnp.float32)
        weighted = dipoles * living[:, None, :]

        def powers(coordinate):
            layers = [jnp.ones_like(coordinate)]
            for degree in range(order - 1):
                layers.append(layers[-1] * coordinate)
            return jnp.stack(layers, axis=1)

        along_x = powers(places[:, 0])
        along_y = powers(places[:, 1])
        along_z = powers(places[:, 2])
        planar = (along_x[:, :, None, :] * along_y[:, None, :, :]).reshape(
            batch_rows, order * order, per_block
        )
        height = (weighted[:, :, None, :] * along_z[:, None, :, :]).reshape(
            batch_rows, 3 * order, per_block
        )
        moment_sums = jnp.einsum(
            "lqp,lrp->lqr", height, planar, precision=lax.Precision.HIGHEST
        ).reshape(batch_rows, -1)
        result = jnp.take(moment_sums, pick_index[0], axis=1) * weight_rows[0][None, :]
        for axis_id in range(1, 3):
            result = (
                result
                + jnp.take(moment_sums, pick_index[axis_id], axis=1) * weight_rows[axis_id][None, :]
            )
        return result

    batches = (
        positions.reshape(total_rows // batch_rows, batch_rows, 3, per_block),
        moments.reshape(total_rows // batch_rows, batch_rows, 3, per_block),
        counts.reshape(total_rows // batch_rows, batch_rows),
    )
    return lax.map(one_batch, batches).reshape(total_rows, -1)


def shards(positions, moments, counts, dest):
    translate = jnp.asarray(shift_table(P_SIZE), jnp.float32)
    coef_count = translate.shape[1]
    narrow_size = lax.axis_size("narrow")
    block_count = positions.shape[0]
    slot_size = block_count // 4
    capacity = narrow_size * slot_size
    per_block = positions.shape[2]
    owners = jnp.arange(narrow_size, dtype=jnp.int32)
    chosen = (dest[:, None] == owners[None, :]).astype(jnp.int32)
    earlier = jnp.sum((jnp.cumsum(chosen, axis=0) - chosen) * chosen, axis=1)
    placing = (dest * slot_size + earlier).astype(jnp.int32)
    tally_in = counts.astype(jnp.float32)

    def bucket(values):
        holder = jnp.zeros((capacity,) + values.shape[1:], values.dtype).at[placing].set(values)
        return holder.reshape((narrow_size, slot_size) + values.shape[1:])

    places = lax.all_to_all(bucket(positions), "narrow", split_axis=0, concat_axis=0, tiled=True)
    dipoles = lax.all_to_all(bucket(moments), "narrow", split_axis=0, concat_axis=0, tiled=True)
    tallies = lax.all_to_all(bucket(tally_in), "narrow", split_axis=0, concat_axis=0, tiled=True)
    senders = tallies.shape[0]
    item_total = tallies.shape[1]
    values = block_moments(
        places.reshape(senders * item_total, 3, per_block),
        dipoles.reshape(senders * item_total, 3, per_block),
        tallies.reshape(-1).astype(jnp.int32),
        P_SIZE,
    )
    arrived = values.reshape(senders, item_total, coef_count)
    filled = (tallies.reshape(capacity) > 0.5).astype(jnp.int32)
    position_in = jnp.cumsum(filled).astype(jnp.int32) - filled
    leaf_total = jnp.sum(filled).astype(jnp.int32)
    target = jnp.where(filled > 0, position_in, capacity)
    leaves = (
        jnp.zeros((capacity, coef_count), jnp.float32)
        .at[target]
        .set(arrived.reshape(capacity, coef_count), mode="drop")
    )
    own_index = lax.axis_index(("wide", "narrow"))
    every_total = lax.all_gather(leaf_total[None], ("wide", "narrow"), axis=0, tiled=True)
    device_ids = jnp.arange(every_total.shape[0], dtype=jnp.int32)
    offset = jnp.sum(jnp.where(device_ids < own_index, every_total, 0)).astype(jnp.int32)
    nonempty = leaf_total > 0
    partial_value = leaves
    first_box = offset
    partials = []
    fragments = []
    passing = []
    last_slots = []
    keeps_first = []
    for level_id in range(1, LEVELS + 1):
        slot_total = (partial_value.shape[0] + 14) // 8
        lead_rows = first_box % 8
        holder = lax.dynamic_update_slice(
            jnp.zeros((slot_total * 8, coef_count), jnp.float32),
            partial_value,
            (lead_rows, jnp.zeros((), jnp.int32)),
        )
        partial_value = jnp.dot(
            holder.reshape(slot_total, 8 * coef_count), translate, precision=lax.Precision.HIGHEST
        )
        first_box = first_box // 8
        box_span = 8**level_id
        split_box = offset % box_span != 0
        last_slot = (offset + leaf_total - 1) // box_span - first_box
        through = jnp.logical_not(nonempty) | split_box & (last_slot == 0)
        fragments.append(partial_value[0] * (split_box & nonempty).astype(jnp.float32))
        passing.append(through.astype(jnp.float32))
        partials.append(partial_value)
        last_slots.append(last_slot)
        keeps_first.append(nonempty & jnp.logical_not(split_box))
    fragment_rows = jnp.stack(fragments)
    pass_flags = jnp.stack(passing)
    every_rows, every_flags = (
        lax.all_gather(fragment_rows[None], ("wide", "narrow"), axis=0, tiled=True),
        lax.all_gather(pass_flags[None], ("wide", "narrow"), axis=0, tiled=True),
    )
    further = (device_ids > own_index).astype(jnp.float32)[:, None]
    blockers = further * (1.0 - every_flags)
    before = jnp.cumsum(blockers, axis=0) - blockers
    reaching = further * (before < 0.5).astype(jnp.float32)
    incoming = jnp.einsum("el,elk->lk", reaching, every_rows, precision=lax.Precision.HIGHEST)
    level_outs = []
    for level_id in range(LEVELS):
        slot_ids = jnp.arange(partials[level_id].shape[0], dtype=jnp.int32)
        taking = (slot_ids == last_slots[level_id]).astype(jnp.float32)[:, None] * (
            1.0 - pass_flags[level_id]
        )
        level_value = partials[level_id] + taking * incoming[level_id][None, :]
        slot_mask = ((slot_ids > 0) | keeps_first[level_id]).astype(jnp.float32)[:, None]
        level_outs.append(level_value * slot_mask)
    return (leaves, jnp.concatenate(level_outs, axis=0))


def solution(mesh):
    placed = (
        P(("wide", "narrow"), None, None),
        P(("wide", "narrow"), None, None),
        P(("wide", "narrow")),
        P(("wide", "narrow")),
    )
    return jax.shard_map(
        shards,
        mesh=mesh,
        in_specs=placed,
        out_specs=(P(("wide", "narrow"), None), P(("wide", "narrow"), None)),
        check_vma=False,
    )
```

profile of v0, /device:TPU:1, one launch (start us, length us, event | category | flops | bytes accessed | tf_op | source)
XLA Modules:
  0.0 440.3 jit_solution(7334072990606004552)
XLA Ops:
  11.5 7.6 %all-to-all-start = ((f32[16,1,8]{2,1,0:T(1,128)}), f32[16,1,8]{2,1,0:T(1,128)S(1)}, u32[]{:S(2)}, u32[]{:S(2)}) async-start(f32[16,1,8]{2,1,0:T(1,128)} %bitcast.2), calls=%async_computation | async-start | bytes 16384 | tf_op jit(solution)/shard_map/all_to_all | solution.py:123
  20.1 1.5 scatter_fusion
  22.5 2.9 all-to-all-done
  25.4 3.8 all-to-all-start.1
  32.5 4.7 %all-to-all-done.1 = f32[16,8,3,256]{3,1,2,0:T(8,128)S(1)} async-done(((f32[16,8,3,256]{3,1,2,0:T(8,128)}), f32[16,8,3,256]{3,1,2,0:T(8,128)S(1)}, u32[]{:S(2)}, u32[]{:S(2)}) %all-to-all-start.1) | async-done | bytes 393248 | tf_op jit(solution)/shard_map/all_to_all | solution.py:122
  37.2 3.6 all-to-all-start.2
  42.1 110.9 %all-reduce = s32[512]{0:T(512)S(1)} all-reduce(s32[512]{0:T(512)S(1)} %dynamic-update-slice), channel_id=1, replica_groups=mesh['wide'=32,'narrow'=16] {'wide','narrow'}, use_global_device_ids=true, to_apply=%add | all-reduce | flops 512 | bytes 4096
  157.6 36.8 %while.11 = (s32[]{:T(128)}, f32[2,64,286]{2,1,0:T(8,128)}, f32[2,64,3,256]{3,1,0,2:T(8,128)S(1)}, s32[2,64]{1,0:T(2,128)S(1)}, f32[2,64,3,256]{3,1,0,2:T(8,128)...) while((s32[]{:T(128)}, f32[2,64,286]{2,1,0:T(8,128)}, ...), condition=%wide.region_7.9_spmd.clone, body=%wide.region_6.8_spmd.sunk.clone.sunk | while | flops 593899904 | bytes 28768708 | solution.py:100
  159.5 11.3 %fusion.118 = f32[64,30,100]{2,1,0:T(8,128)S(1)} fusion(f32[64,100,256]{2,0,1:T(8,128)S(1)} %bitcast.87, f32[64,30,256]{2,0,1:T(8,128)S(1)} %bitcast.88), kind=kOutput, calls=%fused_computation.7.clone.1 | convolution fusion | flops 589824000 | bytes 9287680 | tf_op jit(solution)/shard_map/while/body/eval_jaxpr/lqp,lrp->lqr/dot_general | solution.py:84
  177.8 11.3 %fusion.118 = f32[64,30,100]{2,1,0:T(8,128)S(1)} fusion(f32[64,100,256]{2,0,1:T(8,128)S(1)} %bitcast.87, f32[64,30,256]{2,0,1:T(8,128)S(1)} %bitcast.88), kind=kOutput, calls=%fused_computation.7.clone.1 | convolution fusion | flops 589824000 | bytes 9287680 | tf_op jit(solution)/shard_map/while/body/eval_jaxpr/lqp,lrp->lqr/dot_general | solution.py:84
  194.4 2.2 scatter_custom_fusion.3
  197.3 1.8 dynamic_update_slice.19
  199.0 1.7 reshape.204
  200.8 3.9 fusion.57
  208.8 3.1 fusion.58
  215.4 2.5 fusion.59
  221.3 3.1 fusion.60
  227.8 2.5 fusion.61
  234.0 100.0 %all-reduce.1 = f32[2560]{0:T(1024)S(1)} all-reduce(f32[2560]{0:T(1024)S(1)} %dynamic-update-slice.1), channel_id=2, replica_groups=mesh['wide'=32,'narrow'=16] {'wide','narrow'}, use_global_device_ids=true, to_apply=%add.1 | all-reduce | flops 2560 | bytes 20480
  334.5 1.5 reduce-window.11
  336.9 1.7 copy.78
  338.6 88.6 %all-gather.5.cloned.1.call-done = f32[512,5,286]{2,1,0:T(8,128)} async-done(((f32[1,5,286]{2,1,0:T(8,128)}), f32[512,5,286]{2,1,0:T(8,128)}) %all-gather.5.cloned.1.call-update) | async-done | bytes 2928656 | tf_op jit(solution)/shard_map/all_gather | solution.py:178
  427.2 3.3 multiply_reduce_fusion
  430.9 2.6 concatenate.3
  (179 shorter events, 44.4 us)
Async XLA Ops:
  11.5 13.9 %all-to-all-start = ((f32[16,1,8]{2,1,0:T(1,128)}), f32[16,1,8]{2,1,0:T(1,128)S(1)}, u32[]{:S(2)}, u32[]{:S(2)}) async-start(f32[16,1,8]{2,1,0:T(1,128)} %bitcast.2), calls=%async_computation | async-start | bytes 16384 | tf_op jit(solution)/shard_map/all_to_all | solution.py:123
  21.6 135.9 %copy-start.2 = (f32[286]{0:T(512)S(1)}, f32[286]{0:T(512)}, u32[]{:S(2)}) copy-start(f32[286]{0:T(512)} %constant.466) | copy-start | bytes 3436
  21.6 135.9 %copy-start.3 = (f32[286]{0:T(512)S(1)}, f32[286]{0:T(512)}, u32[]{:S(2)}) copy-start(f32[286]{0:T(512)} %constant.467) | copy-start | bytes 3436
  21.6 135.9 %copy-start.4 = (f32[286]{0:T(512)S(1)}, f32[286]{0:T(512)}, u32[]{:S(2)}) copy-start(f32[286]{0:T(512)} %constant.468) | copy-start | bytes 3436
  21.6 135.9 %copy-start.5 = (s32[286]{0:T(512)S(1)}, s32[286]{0:T(512)}, u32[]{:S(2)}) copy-start(s32[286]{0:T(512)} %constant.465) | copy-start | bytes 3436
  21.7 135.9 %copy-start.6 = (s32[286]{0:T(512)S(1)}, s32[286]{0:T(512)}, u32[]{:S(2)}) copy-start(s32[286]{0:T(512)} %constant.463) | copy-start | bytes 3436
  21.7 135.9 %copy-start.7 = (s32[286]{0:T(512)S(1)}, s32[286]{0:T(512)}, u32[]{:S(2)}) copy-start(s32[286]{0:T(512)} %constant.464) | copy-start | bytes 3436
  25.4 11.8 %all-to-all-start.1 = ((f32[16,8,3,256]{3,1,2,0:T(8,128)}), f32[16,8,3,256]{3,1,2,0:T(8,128)S(1)}, u32[]{:S(2)}, u32[]{:S(2)}) async-start(f32[16,8,3,256]{3,1,2,0:T(8,128)} %copy.66), calls=%async_computation.1 | async-start | bytes 786432 | tf_op jit(solution)/shard_map/all_to_all | solution.py:122
  37.2 120.3 %all-to-all-start.2 = ((f32[16,8,3,256]{3,1,2,0:T(8,128)}), f32[16,8,3,256]{3,1,2,0:T(8,128)S(1)}, u32[]{:S(2)}, u32[]{:S(2)}) async-start(f32[16,8,3,256]{3,1,2,0:T(8,128)} %copy.69), calls=%async_computation.2 | async-start | bytes 786432 | tf_op jit(solution)/shard_map/all_to_all | solution.py:121
  40.7 386.5 %all-gather.5.cloned.1.call-start = ((), (), s32[]{:S(2)}) async-start(), calls=%async_computation.3 | async-start | bytes 6303744 | tf_op jit(solution)/shard_map/all_gather | solution.py:178
  194.4 14.5 %copy-start = (f32[2288,286]{1,0:T(8,128)S(1)}, f32[2288,286]{1,0:T(8,128)}, u32[]{:S(2)}) copy-start(f32[2288,286]{1,0:T(8,128)} %constant.247.clone) | copy-start | bytes 7852420
  227.8 3.2 copy-start.8
  230.3 0.7 copy-start.10
  336.9 93.7 %copy-start.1 = (f32[3,286]{1,0:T(4,128)S(1)}, f32[3,286]{1,0:T(4,128)}, u32[]{:S(2)}) copy-start(f32[3,286]{1,0:T(4,128)} %fusion.58) | copy-start | bytes 10300
  336.9 93.9 %copy-start.9 = (f32[2,286]{1,0:T(2,128)S(1)}, f32[2,286]{1,0:T(2,128)}, u32[]{:S(2)}) copy-start(f32[2,286]{1,0:T(2,128)} %fusion.60) | copy-start | bytes 6868
  336.9 93.9 %copy-start.11 = (f32[2,286]{1,0:T(2,128)S(1)}, f32[2,286]{1,0:T(2,128)}, u32[]{:S(2)}) copy-start(f32[2,286]{1,0:T(2,128)} %copy-done.10) | copy-start | bytes 6868
Sparse Core Ops, SparseCore 0:
  232.5 194.7 all-gather.4
where the time goes:
time: 442 us; the launch traced here: 440 us
  blocking collectives  211 us (48%)
  waiting for transfers between devices  96.2 us (22%)
  local copies, waits for them, and re-layouts  45.8 us (10%)
  matrix products  37.8 us (9%)
  between operations  19.2 us (4%)
  starting transfers between devices  14.9 us (3%)
  other arithmetic  14.7 us (3%)
    unnamed x2, blocking collectives  211 us
    all_gather x1, waiting for transfers between devices, shards(): lax.all_gather(fragment_rows[None], ('wide', 'narrow'), axis=0, tiled=True)  88.6 us
    dot_general x2, matrix products, one_batch(): jnp.einsum('lqp,lrp->lqr', height, planar, precision=lax.Precision.HIGHEST)  22.6 us
    dot_general x5, matrix products, shards(): jnp.dot(holder.reshape(slot_total, 8 * coef_count), translate, precision=...  15.2 us
  transfers between devices with their start and end apart: 4, of which 3 were waited for; matrix products, arithmetic and copies ran while one was open for 3% of the time, Pallas kernels for 0%

commit v1 on v0

v1 whole, which is shorter than its diff:
```python
import math

import jax
import jax.numpy as jnp
import numpy as np
from jax import lax
from jax.experimental import pallas as pl
from jax.experimental.pallas import tpu as pltpu
from jax.sharding import PartitionSpec as P

P_SIZE = 10
COEFS = 286
GROUP = 512
F32 = jnp.float32
BF16 = jnp.bfloat16


def exponent_list(order):
    triples = []
    for degree in range(order + 1):
        for power_x in range(degree, -1, -1):
            for power_y in range(degree - power_x, -1, -1):
                triples.append((power_x, power_y, degree - power_x - power_y))
    return triples


def tables():
    triples = exponent_list(P_SIZE)
    shift = np.zeros((256, 384), np.float32)
    for column, target in enumerate(triples):
        for row, source in enumerate(triples[:256]):
            if all(s <= t for s, t in zip(source, target)):
                shift[row, column] = 0.5 ** sum(target) * math.prod(
                    math.comb(t, s) for s, t in zip(source, target)
                )
    signs = np.ones((8, 384), np.float32)
    for octant in range(8):
        for column, target in enumerate(triples):
            for axis in range(3):
                if not (octant >> axis) & 1 and target[axis] % 2:
                    signs[octant, column] = -signs[octant, column]
    return shift, signs


def split(value):
    high = value.astype(BF16)
    return high, (value - high.astype(F32)).astype(BF16)


def moments_kernel(places_ref, dipoles_ref, counts_ref, dest_ref, out_ref, grid_ref, sums_ref):
    index_of = {triple: i for i, triple in enumerate(exponent_list(P_SIZE))}

    def turned(values):
        quarters = [values[:, 64 * q : 64 * q + 64] for q in range(4)]
        return jnp.concatenate(quarters, axis=0).T

    live = jnp.concatenate([counts_ref[...]] * 4, axis=1)
    rows = lax.broadcasted_iota(jnp.int32, (64, 128), 0)
    lanes = lax.broadcasted_iota(jnp.int32, (64, 128), 1)
    living = rows + 64 * (lanes // 32) < live
    for axis in range(3):
        grid_ref[axis] = turned(places_ref[axis])
        grid_ref[3 + axis] = jnp.where(living, turned(dipoles_ref[axis]), 0.0)
    sums_ref[...] = jnp.zeros(sums_ref.shape, F32)

    def half(step, carry):
        picked = pl.ds(pl.multiple_of(step * 32, 32), 32)
        x, y, z, mx, my, mz = [grid_ref[k, picked, :] for k in range(6)]

        def note(triple, psi):
            folded = (psi[0:8] + psi[8:16]) + (psi[16:24] + psi[24:32])
            sums_ref[index_of[triple]] += folded

        phi_x, psi_x = None, None
        for a in range(P_SIZE + 1):
            if a == 1:
                phi_x, psi_x = x, mx
            elif a > 1:
                phi_x, psi_x = phi_x * x, psi_x * x + mx * phi_x
            phi_y, psi_y = phi_x, psi_x
            for e in range(P_SIZE + 1 - a):
                if e > 0:
                    if phi_y is None:
                        phi_y, psi_y = y, my
                    elif psi_y is None:
                        phi_y, psi_y = phi_y * y, my * phi_y
                    else:
                        phi_y, psi_y = phi_y * y, psi_y * y + my * phi_y
                phi, psi = phi_y, psi_y
                for c in range(P_SIZE + 1 - a - e):
                    if c > 0:
                        if phi is None:
                            phi, psi = z, mz
                        else:
                            phi, psi = phi * z, psi * z + mz * phi
                    if psi is not None:
                        note((a, e, c), psi)
        return carry

    lax.fori_loop(0, 2, half, 0)
    folded = jnp.sum(sums_ref[...], axis=1)
    blank = jnp.zeros((1, 96), F32)
    where_to = jnp.concatenate([dest_ref[...].astype(F32), blank], axis=1)
    row = lax.broadcasted_iota(jnp.int32, folded.shape, 0)
    folded = jnp.where(row == COEFS, where_to, folded * (1.0 / 16.0))
    folded = jnp.concatenate([folded, jnp.zeros((96, 128), F32)], axis=0).T
    values = (folded[0:32] + folded[32:64]) + (folded[64:96] + folded[96:128])
    out_ref[0:32] = values[:, 0:128]
    out_ref[32:64] = values[:, 128:256]
    tail = values[:, 256:288]
    out_ref[64:72] = jnp.concatenate([tail[8 * g : 8 * g + 8] for g in range(4)], axis=1)


def tree_kernel(
    where_ref, got_ref, shift_ref, signs_ref, leaf_ref, box_ref, send_ref, own_ref
):
    me = where_ref[0]
    group = where_ref[1]
    lane = lax.broadcasted_iota(jnp.int32, (128, 128), 1)
    tails = got_ref[:, 64:72, :].reshape(128, 128)
    turned = tails.T
    dest_row = jnp.concatenate([turned[32 * g + 30 : 32 * g + 31] for g in range(4)], axis=1)
    spot = lax.broadcasted_iota(jnp.int32, (1, GROUP), 1)
    block_row = ((spot // 8) % 16) * 32 + (spot // 128) * 8 + spot % 8
    key_row = dest_row * 512.0 + block_row.astype(F32)
    spot = lax.broadcasted_iota(jnp.int32, (128, 1), 0)
    high_parts, low_parts, pair_parts, key_parts = [], [], [], []
    for g in range(4):
        tail = tails if g == 0 else pltpu.roll(tails, 128 - 32 * g, 1)
        block = (spot // 8) * 32 + g * 8 + spot % 8
        key_parts.append(tail[:, 30:31] * 512.0 + block.astype(F32))
        first = got_ref[:, 8 * g : 8 * g + 8, :].reshape(128, 128)
        second = got_ref[:, 32 + 8 * g : 40 + 8 * g, :].reshape(128, 128)
        tail = jnp.where(lane < 30, tail, 0.0)
        top = tail.astype(BF16).astype(F32)
        pair = top + pltpu.roll(tail - top, 32, 1)
        (first_high, first_low), (second_high, second_low) = split(first), split(second)
        high_parts.append(jnp.concatenate([first_high, second_high], axis=1))
        low_parts.append(jnp.concatenate([first_low, second_low], axis=1))
        pair_parts.append(pair.astype(BF16))
    held = jnp.concatenate(
        [
            jnp.concatenate(high_parts, axis=0),
            jnp.concatenate(low_parts, axis=0),
            jnp.concatenate(pair_parts, axis=0),
        ],
        axis=1,
    )
    smaller = jnp.zeros((8, GROUP), F32)
    for g in range(4):
        less = jnp.where(key_parts[g] < key_row, 1.0, 0.0)
        smaller = smaller + jnp.sum(less.reshape(16, 8, GROUP), axis=0)
    rank = jnp.sum(smaller, axis=0, keepdims=True).astype(jnp.int32)
    mine = me.astype(F32)
    start = jnp.sum(jnp.where(dest_row < mine, 1.0, 0.0), axis=1, keepdims=True).astype(jnp.int32)
    tally = jnp.sum(jnp.where(dest_row == mine, 1.0, 0.0), axis=1, keepdims=True).astype(jnp.int32)
    row = lax.broadcasted_iota(jnp.int32, (GROUP, 1), 0)
    turned_row = (row % 8) * 64 + ((row // 8) % 8) * 8 + row // 64
    slot = lax.broadcasted_iota(jnp.int32, (128, 1), 0)
    wanted = jnp.concatenate([turned_row, jnp.where(slot < tally, start + slot, -1)], axis=0)
    chosen = jnp.where(wanted == rank, 1.0, 0.0).astype(BF16)
    placed = jnp.dot(chosen, held, preferred_element_type=F32)
    own = placed[GROUP:]
    leaf_first = (own[:, 0:128] + own[:, 256:384]).T
    leaf_second = (own[:, 128:256] + own[:, 384:512]).T
    own_tail = own[:, 512:640]
    leaf_tail = (own_tail + pltpu.roll(own_tail, 96, 1)).T
    leaf_ref[0:128] = leaf_first
    leaf_ref[128:256] = leaf_second
    leaf_ref[256:COEFS] = leaf_tail[0 : COEFS - 256]

    shift = shift_ref[...]
    tiny = 2.0**-P_SIZE

    def moved(high, low):
        stacked = jnp.dot(
            jnp.concatenate([high, low], axis=0), shift, preferred_element_type=F32
        )
        count = high.shape[0]
        return stacked[:count] + stacked[count:]

    def signed(octant):
        return signs_ref[octant : octant + 1, :]

    sign_rows = jnp.concatenate(
        [jnp.broadcast_to(signed(o)[:, 0:256], (64, 256)) for o in range(8)], axis=0
    )
    sons = placed[:GROUP]
    high = (sons[:, 0:256] * sign_rows).astype(BF16)
    low = (sons[:, 256:512] * sign_rows).astype(BF16)
    parts = moved(high, low)
    level = parts[0:64] * signed(0)
    tail_sum = sons[0:64, 512:640]
    for o in range(1, 8):
        level = level + parts[64 * o : 64 * o + 64] * signed(o)
        tail_sum = tail_sum + sons[64 * o : 64 * o + 64, 512:640]
    tail_lane = lax.broadcasted_iota(jnp.int32, (1, 128), 1) < 30

    def with_tail(body, tail):
        added = body[:, 256:384] + jnp.where(tail_lane, tail * tiny, 0.0)
        return jnp.concatenate([body[:, 0:256], added], axis=1)

    level_1 = with_tail(level, tail_sum + pltpu.roll(tail_sum, 96, 1))
    sign_rows = jnp.concatenate(
        [jnp.broadcast_to(signed(o), (8, 384)) for o in range(8)], axis=0
    )
    parts = moved(*split(level_1[:, 0:256] * sign_rows[:, 0:256])) * sign_rows
    level = jnp.sum(parts.reshape(8, 8, 384), axis=0)
    tail_sum = jnp.sum(level_1[:, 256:384].reshape(8, 8, 128), axis=0)
    level_2 = with_tail(level, tail_sum)
    all_signs = signs_ref[...]
    parts = moved(*split(level_2[:, 0:256] * all_signs[:, 0:256])) * all_signs
    level = jnp.sum(parts, axis=0, keepdims=True)
    tail_sum = jnp.sum(level_2[:, 256:384], axis=0, keepdims=True)
    level_3 = with_tail(level, tail_sum)
    sublane = lax.broadcasted_iota(jnp.int32, (8, 384), 0)

    def share(value, octant):
        sign = jnp.sum(jnp.where(sublane == octant, all_signs, 0.0), axis=0, keepdims=True)
        eight = jnp.broadcast_to(value * sign, (8, 384))
        part = moved(*split(eight[:, 0:256]))[0:1] * sign
        return with_tail(part, value[:, 256:384])

    level_4 = share(level_3, group % 8)
    level_5 = share(level_4, group // 8)
    send_ref[0:1] = level_4[:, 0:128]
    send_ref[1:2] = level_4[:, 128:256]
    send_ref[2:3] = level_4[:, 256:384]
    send_ref[3:4] = level_5[:, 0:128]
    send_ref[4:5] = level_5[:, 128:256]
    send_ref[5:6] = level_5[:, 256:384]
    send_ref[6:8] = jnp.zeros((2, 128), F32)

    boxes = jnp.concatenate(
        [level_1, level_2, level_3, jnp.zeros((55, 384), F32)], axis=0
    )
    end = start + tally
    out_slot = lax.broadcasted_iota(jnp.int32, (32, 1), 0)
    box_1 = start // 8 + out_slot
    box_2 = start // 64 + out_slot - 17
    source = jnp.where((box_1 * 8 >= start) & (box_1 * 8 < end), (box_1 % 8) * 8 + box_1 // 8, -1)
    source_2 = jnp.where((box_2 * 64 >= start) & (box_2 * 64 < end), 64 + box_2, -1)
    first_of_group = (start == 0) & (tally > 0)
    source_3 = jnp.where(first_of_group & (out_slot == 20), 72, -1)
    source = jnp.where(out_slot < 17, source, jnp.where(out_slot < 20, source_2, source_3))
    column = lax.broadcasted_iota(jnp.int32, (32, 128), 1)
    select = jnp.where(column == source, 1.0, 0.0).astype(BF16)
    high, low = split(boxes)
    picked = jnp.dot(select, high, preferred_element_type=F32) + jnp.dot(
        select, low, preferred_element_type=F32
    )
    box_ref[...] = picked[0:26, 0:COEFS]
    heads = first_of_group & (lax.broadcasted_iota(jnp.int32, (8, 128), 0) >= 0)
    own_ref[...] = jnp.where(heads, 1.0, 0.0)


def finish_kernel(where_ref, own_ref, four_ref, five_ref, part_ref, box_ref):
    group = where_ref[1]
    own = own_ref[0:1]
    keep_4 = own * jnp.where(group % 8 == 0, 1.0, 0.0)
    keep_5 = own * jnp.where(group == 0, 1.0, 0.0)
    box_ref[...] = part_ref[...]
    for at, keep, ref, base in ((22, keep_4, four_ref, 0), (24, keep_5, five_ref, 3)):
        box_ref[at : at + 1, 0:128] = ref[base : base + 1] * keep
        box_ref[at : at + 1, 128:256] = ref[base + 1 : base + 2] * keep
        last = ref[base + 2 : base + 3] * keep
        box_ref[at : at + 1, 256:COEFS] = last[:, 0 : COEFS - 256]


VMEM = pl.BlockSpec(memory_space=pltpu.VMEM)
SMEM = pl.BlockSpec(memory_space=pltpu.SMEM)
PARAMS = pltpu.CompilerParams(vmem_limit_bytes=40 * 1024 * 1024)


def shards(positions, moments, counts, dest):
    shift, signs = tables()
    where = jnp.stack([lax.axis_index("narrow"), lax.axis_index("wide")]).astype(jnp.int32)
    sent = pl.pallas_call(
        moments_kernel,
        out_shape=jax.ShapeDtypeStruct((72, 128), F32),
        in_specs=[VMEM] * 4,
        out_specs=VMEM,
        scratch_shapes=[pltpu.VMEM((6, 64, 128), F32), pltpu.VMEM((288, 8, 128), F32)],
        compiler_params=PARAMS,
    )(
        jnp.transpose(positions, (1, 0, 2)),
        jnp.transpose(moments, (1, 0, 2)),
        counts.reshape(1, 32),
        dest.reshape(1, 32),
    )
    got = lax.all_to_all(
        jnp.broadcast_to(sent[None], (16, 72, 128)), "narrow", split_axis=0, concat_axis=0, tiled=True
    )
    leaf, box, share, own = pl.pallas_call(
        tree_kernel,
        out_shape=(
            jax.ShapeDtypeStruct((COEFS, 128), F32),
            jax.ShapeDtypeStruct((26, COEFS), F32),
            jax.ShapeDtypeStruct((8, 128), F32),
            jax.ShapeDtypeStruct((8, 128), F32),
        ),
        in_specs=[SMEM, VMEM, VMEM, VMEM],
        out_specs=(VMEM,) * 4,
        compiler_params=PARAMS,
    )(where, got, jnp.asarray(shift, BF16), jnp.asarray(signs, F32))
    pair = share + lax.ppermute(share, "wide", [(2 * i + 1, 2 * i) for i in range(16)])
    quad = pair
    for j in (2, 4, 6):
        quad = quad + lax.ppermute(pair, "wide", [(8 * q + j, 8 * q) for q in range(4)])
    top = quad
    for j in (24, 16, 8):
        top = top + lax.ppermute(quad, "wide", [(j, 0)])
    box = pl.pallas_call(
        finish_kernel,
        out_shape=jax.ShapeDtypeStruct((26, COEFS), F32),
        in_specs=[SMEM, VMEM, VMEM, VMEM, VMEM],
        out_specs=VMEM,
        compiler_params=PARAMS,
    )(where, own, quad, top, box)
    return leaf.T, box


def solution(mesh):
    both = ("wide", "narrow")
    placed = (P(both, None, None), P(both, None, None), P(both), P(both))
    return jax.shard_map(
        shards,
        mesh=mesh,
        in_specs=placed,
        out_specs=(P(both, None), P(both, None)),
        check_vma=False,
    )
```

time: 442 us -> 56.9 us (0.13)
  the two profiles are of different devices: /device:TPU:1 before, /device:TPU:8 now
where the time goes in v1:
time: 56.9 us; the launch traced here: 56.5 us
  waiting for transfers between devices  27.9 us (49%)
  starting transfers between devices  18.3 us (32%)
  Pallas kernels  6.11 us (11%)
  local copies, waits for them, and re-layouts  3.31 us (6%)
  between operations  0.73 us (1%)
    ppermute x3, waiting for transfers between devices, shards(): top = top + lax.ppermute(quad, 'wide', [(j, 0)])  12.9 us
    all_to_all x1, starting transfers between devices, shards(): lax.all_to_all(jnp.broadcast_to(sent[None], (16, 72, 128)), 'narrow', spl...  9.32 us
    all_to_all x1, waiting for transfers between devices, shards(): lax.all_to_all(jnp.broadcast_to(sent[None], (16, 72, 128)), 'narrow', spl...  9.08 us
    ppermute x3, waiting for transfers between devices, shards(): lax.ppermute(pair, 'wide', [(8 * q + j, 8 * q) for q in range(4)])  4.2 us
    ppermute x3, starting transfers between devices, shards(): lax.ppermute(pair, 'wide', [(8 * q + j, 8 * q) for q in range(4)])  3.86 us
    ppermute x3, starting transfers between devices, shards(): top = top + lax.ppermute(quad, 'wide', [(j, 0)])  3.86 us
    pallas_call x1, Pallas kernels, shards(): pl.pallas_call(tree_kernel, out_shape=(jax.ShapeDtypeStruct((COEFS, 128),...  2.93 us
    unnamed x12, local copies, waits for them, and re-layouts  2.45 us
  transfers between devices with their start and end apart: 8, of which 7 were waited for; matrix products, arithmetic and copies ran while one was open for 0% of the time, Pallas kernels for 0%

profile of v1, /device:TPU:8, one launch (start us, length us, event | category | flops | bytes accessed | tf_op | source)
XLA Modules:
  0.0 56.5 jit_solution(17775756257440639908)
XLA Ops:
  0.7 0.6 %copy-done.4 = s32[32]{0:T(128)S(1)} copy-done((s32[32]{0:T(128)S(1)}, s32[32]{0:T(128)}, u32[]{:S(2)}) %copy-start.4) | copy-done | bytes 152
  1.3 0.0 copy-done.5
  1.3 0.9 %copy-done.1 = f32[32,3,256]{2,0,1:T(8,128)S(1)} copy-done((f32[32,3,256]{2,0,1:T(8,128)S(1)}, f32[32,3,256]{2,0,1:T(8,128)}, u32[]{:S(2)}) %copy-start.1) | copy-done | bytes 98328
  2.2 0.9 %copy-done.2 = f32[32,3,256]{2,0,1:T(8,128)S(1)} copy-done((f32[32,3,256]{2,0,1:T(8,128)S(1)}, f32[32,3,256]{2,0,1:T(8,128)}, u32[]{:S(2)}) %copy-start.2) | copy-done | bytes 98328
  3.1 2.0 %shard_map.77 = f32[72,128]{1,0:T(8,128)S(1)} custom-call(f32[3,32,256]{2,1,0:T(8,128)S(1)} %bitcast.7, f32[3,32,256]{2,1,0:T(8,128)S(1)} %bitcast.8, s32[1,32]{1,0:T(1,128)S(1)} %bitcast.9, s32[1,32]{1,0:T(1,128)S(1)} %bitcast.10), custom_call_target="tpu_custom_call" | custom-call | tf_op jit(solution)/shard_map/pallas_call | solution.py:278
  5.1 0.9 %broadcast_in_dim.2 = f32[16,72,128]{2,1,0:T(8,128)} broadcast(f32[72,128]{1,0:T(8,128)S(1)} %shard_map.77), dimensions={1,2} | broadcast | bytes 626688 | tf_op jit(solution)/shard_map/broadcast_in_dim | solution.py:292
  6.0 9.3 %all-to-all-start = ((f32[16,72,128]{2,1,0:T(8,128)}), f32[16,72,128]{2,1,0:T(8,128)S(1)}, u32[]{:S(2)}, u32[]{:S(2)}) async-start(f32[16,72,128]{2,1,0:T(8,128)} %broadcast_in_dim.2), calls=%async_computation | async-start | bytes 1179648 | tf_op jit(solution)/shard_map/all_to_all | solution.py:291
  15.3 0.1 pad_add_fusion.where_ref
  15.4 9.1 %all-to-all-done.got_ref = f32[16,72,128]{2,1,0:T(8,128)S(1)} async-done(((f32[16,72,128]{2,1,0:T(8,128)}), f32[16,72,128]{2,1,0:T(8,128)S(1)}, u32[]{:S(2)}, u32[]{:S(2)}) %all-to-all-start) | async-done | bytes 589856 | tf_op jit(solution)/shard_map/all_to_all | solution.py:291
  24.5 2.9 %shard_map.78 = (f32[286,128]{1,0:T(8,128)}, f32[26,286]{1,0:T(8,128)S(1)}, f32[8,128]{1,0:T(8,128)S(1)}, f32[8,128]{1,0:T(8,128)S(1)}) custom-call(s32[2]{0:T(128)S(1)} %pad_add_fusion.where_ref, f32[16,72,128]{2,1,0:T(8,128)S(1)} %all-to-all-done.got_ref, bf16[256,384]{1,0:T(8,128)(2,1)S(1)} %copy-done, f32[8,384]{1,0:T(8,128)S(1)} %copy-done.3), custom_call_target="tpu_custom_call" | custom-call | tf_op jit(solution)/shard_map/pallas_call | solution.py:294
  27.4 1.3 %collective-permute-start = (f32[8,128]{1,0:T(8,128)S(1)}, f32[8,128]{1,0:T(8,128)S(1)}, u32[]{:S(2)}, u32[]{:S(2)}) collective-permute-start(f32[8,128]{1,0:T(8,128)S(1)} %get-tuple-element.8), channel_id=1, source_target_pairs={{16,0},{48,32},{80,64},{112,96},{144,128},{176,160},{208,192},{240... | collective-permute-start | bytes 12296 | tf_op jit(solution)/shard_map/ppermute | solution.py:306
  28.7 1.8 %collective-permute-done = f32[8,128]{1,0:T(8,128)S(1)} collective-permute-done((f32[8,128]{1,0:T(8,128)S(1)}, f32[8,128]{1,0:T(8,128)S(1)}, u32[]{:S(2)}, u32[]{:S(2)}) %collective-permute-start) | collective-permute-done | bytes 4128 | tf_op jit(solution)/shard_map/ppermute | solution.py:306
  30.5 1.3 %collective-permute-start.3 = (f32[8,128]{1,0:T(8,128)S(1)}, f32[8,128]{1,0:T(8,128)S(1)}, u32[]{:S(2)}, u32[]{:S(2)}) collective-permute-start(f32[8,128]{1,0:T(8,128)S(1)} %add.21), channel_id=1, source_target_pairs={{96,0},{224,128},{352,256},{480,384},{97,1},{225,129},{353,257},{4... | collective-permute-start | bytes 12296 | tf_op jit(solution)/shard_map/ppermute | solution.py:309
  31.7 1.3 %collective-permute-start.2 = (f32[8,128]{1,0:T(8,128)S(1)}, f32[8,128]{1,0:T(8,128)S(1)}, u32[]{:S(2)}, u32[]{:S(2)}) collective-permute-start(f32[8,128]{1,0:T(8,128)S(1)} %add.21), channel_id=1, source_target_pairs={{64,0},{192,128},{320,256},{448,384},{65,1},{193,129},{321,257},{4... | collective-permute-start | bytes 12296 | tf_op jit(solution)/shard_map/ppermute | solution.py:309
  33.0 1.3 %collective-permute-start.1 = (f32[8,128]{1,0:T(8,128)S(1)}, f32[8,128]{1,0:T(8,128)S(1)}, u32[]{:S(2)}, u32[]{:S(2)}) collective-permute-start(f32[8,128]{1,0:T(8,128)S(1)} %add.21), channel_id=1, source_target_pairs={{32,0},{160,128},{288,256},{416,384},{33,1},{161,129},{289,257},{4... | collective-permute-start | bytes 12296 | tf_op jit(solution)/shard_map/ppermute | solution.py:309
  34.3 3.4 %collective-permute-done.3 = f32[8,128]{1,0:T(8,128)S(1)} collective-permute-done((f32[8,128]{1,0:T(8,128)S(1)}, f32[8,128]{1,0:T(8,128)S(1)}, u32[]{:S(2)}, u32[]{:S(2)}) %collective-permute-start.3) | collective-permute-done | bytes 4128 | tf_op jit(solution)/shard_map/ppermute | solution.py:309
  37.7 0.4 collective-permute-done.2
  38.1 0.4 collective-permute-done.1
  38.6 1.3 %collective-permute-start.6 = (f32[8,128]{1,0:T(8,128)S(1)}, f32[8,128]{1,0:T(8,128)S(1)}, u32[]{:S(2)}, u32[]{:S(2)}) collective-permute-start(f32[8,128]{1,0:T(8,128)S(1)} %add_add_fusion.1.four_ref), channel_id=1, source_target_pairs={{128,0},{129,1},{130,2},{131,3},{132,4},{133,5},{134,6},{135,7},{1... | collective-permute-start | bytes 12296 | tf_op jit(solution)/shard_map/ppermute | solution.py:312
  39.8 1.3 %collective-permute-start.5 = (f32[8,128]{1,0:T(8,128)S(1)}, f32[8,128]{1,0:T(8,128)S(1)}, u32[]{:S(2)}, u32[]{:S(2)}) collective-permute-start(f32[8,128]{1,0:T(8,128)S(1)} %add_add_fusion.1.four_ref), channel_id=1, source_target_pairs={{256,0},{257,1},{258,2},{259,3},{260,4},{261,5},{262,6},{263,7},{2... | collective-permute-start | bytes 12296 | tf_op jit(solution)/shard_map/ppermute | solution.py:312
  41.1 1.3 %collective-permute-start.4 = (f32[8,128]{1,0:T(8,128)S(1)}, f32[8,128]{1,0:T(8,128)S(1)}, u32[]{:S(2)}, u32[]{:S(2)}) collective-permute-start(f32[8,128]{1,0:T(8,128)S(1)} %add_add_fusion.1.four_ref), channel_id=1, source_target_pairs={{384,0},{385,1},{386,2},{387,3},{388,4},{389,5},{390,6},{391,7},{3... | collective-permute-start | bytes 12296 | tf_op jit(solution)/shard_map/ppermute | solution.py:312
  42.4 5.6 %collective-permute-done.6 = f32[8,128]{1,0:T(8,128)S(1)} collective-permute-done((f32[8,128]{1,0:T(8,128)S(1)}, f32[8,128]{1,0:T(8,128)S(1)}, u32[]{:S(2)}, u32[]{:S(2)}) %collective-permute-start.6) | collective-permute-done | bytes 4128 | tf_op jit(solution)/shard_map/ppermute | solution.py:312
  48.0 7.3 %collective-permute-done.5 = f32[8,128]{1,0:T(8,128)S(1)} collective-permute-done((f32[8,128]{1,0:T(8,128)S(1)}, f32[8,128]{1,0:T(8,128)S(1)}, u32[]{:S(2)}, u32[]{:S(2)}) %collective-permute-start.5) | collective-permute-done | bytes 4128 | tf_op jit(solution)/shard_map/ppermute | solution.py:312
  55.3 1.2 %shard_map.79 = f32[26,286]{1,0:T(8,128)} custom-call(s32[2]{0:T(128)S(1)} %pad_add_fusion.where_ref, f32[8,128]{1,0:T(8,128)S(1)} %get-tuple-element.7.own_ref, f32[8,128]{1,0:T(8,128)S(1)} %add_add_fusion.1.four_ref, f32[8,128]{1,0:T(8,128)S(1)} %add_add_fusion.five_ref, f32[26,286]{1,0:T(8,128)S(1)} %get-tuple-element.9.part_ref), custom_call_target="tpu_custom_call" | custom-call | tf_op jit(solution)/shard_map/pallas_call | solution.py:313
  (12 shorter events, 0.0 us)
Async XLA Ops:
  0.6 0.7 %copy-start.4 = (s32[32]{0:T(128)S(1)}, s32[32]{0:T(128)}, u32[]{:S(2)}) copy-start(s32[32]{0:T(128)} %param.8) | copy-start | bytes 388
  0.6 0.7 %copy-start.5 = (s32[32]{0:T(128)S(1)}, s32[32]{0:T(128)}, u32[]{:S(2)}) copy-start(s32[32]{0:T(128)} %param.9) | copy-start | bytes 388
  1.3 0.9 %copy-start.1 = (f32[32,3,256]{2,0,1:T(8,128)S(1)}, f32[32,3,256]{2,0,1:T(8,128)}, u32[]{:S(2)}) copy-start(f32[32,3,256]{2,0,1:T(8,128)} %param.6) | copy-start | bytes 294916
  2.2 0.9 %copy-start.2 = (f32[32,3,256]{2,0,1:T(8,128)S(1)}, f32[32,3,256]{2,0,1:T(8,128)}, u32[]{:S(2)}) copy-start(f32[32,3,256]{2,0,1:T(8,128)} %param.7) | copy-start | bytes 294916
  6.0 18.5 %copy-start = (bf16[256,384]{1,0:T(8,128)(2,1)S(1)}, bf16[256,384]{1,0:T(8,128)(2,1)}, u32[]{:S(2)}) copy-start(bf16[256,384]{1,0:T(8,128)(2,1)} %constant.13.clone.shift_ref) | copy-start | bytes 589828
  6.0 18.5 %all-to-all-start = ((f32[16,72,128]{2,1,0:T(8,128)}), f32[16,72,128]{2,1,0:T(8,128)S(1)}, u32[]{:S(2)}, u32[]{:S(2)}) async-start(f32[16,72,128]{2,1,0:T(8,128)} %broadcast_in_dim.2), calls=%async_computation | async-start | bytes 1179648 | tf_op jit(solution)/shard_map/all_to_all | solution.py:291
  15.3 9.2 %copy-start.3 = (f32[8,384]{1,0:T(8,128)S(1)}, f32[8,384]{1,0:T(8,128)}, u32[]{:S(2)}) copy-start(f32[8,384]{1,0:T(8,128)} %constant.14.clone.signs_ref) | copy-start | bytes 36868
  27.4 3.0 %collective-permute-start = (f32[8,128]{1,0:T(8,128)S(1)}, f32[8,128]{1,0:T(8,128)S(1)}, u32[]{:S(2)}, u32[]{:S(2)}) collective-permute-start(f32[8,128]{1,0:T(8,128)S(1)} %get-tuple-element.8), channel_id=1, source_target_pairs={{16,0},{48,32},{80,64},{112,96},{144,128},{176,160},{208,192},{240... | collective-permute-start | bytes 12296 | tf_op jit(solution)/shard_map/ppermute | solution.py:306
  30.5 7.3 %collective-permute-start.3 = (f32[8,128]{1,0:T(8,128)S(1)}, f32[8,128]{1,0:T(8,128)S(1)}, u32[]{:S(2)}, u32[]{:S(2)}) collective-permute-start(f32[8,128]{1,0:T(8,128)S(1)} %add.21), channel_id=1, source_target_pairs={{96,0},{224,128},{352,256},{480,384},{97,1},{225,129},{353,257},{4... | collective-permute-start | bytes 12296 | tf_op jit(solution)/shard_map/ppermute | solution.py:309
  31.7 6.4 %collective-permute-start.2 = (f32[8,128]{1,0:T(8,128)S(1)}, f32[8,128]{1,0:T(8,128)S(1)}, u32[]{:S(2)}, u32[]{:S(2)}) collective-permute-start(f32[8,128]{1,0:T(8,128)S(1)} %add.21), channel_id=1, source_target_pairs={{64,0},{192,128},{320,256},{448,384},{65,1},{193,129},{321,257},{4... | collective-permute-start | bytes 12296 | tf_op jit(solution)/shard_map/ppermute | solution.py:309
  33.0 5.5 %collective-permute-start.1 = (f32[8,128]{1,0:T(8,128)S(1)}, f32[8,128]{1,0:T(8,128)S(1)}, u32[]{:S(2)}, u32[]{:S(2)}) collective-permute-start(f32[8,128]{1,0:T(8,128)S(1)} %add.21), channel_id=1, source_target_pairs={{32,0},{160,128},{288,256},{416,384},{33,1},{161,129},{289,257},{4... | collective-permute-start | bytes 12296 | tf_op jit(solution)/shard_map/ppermute | solution.py:309
  38.6 9.5 %collective-permute-start.6 = (f32[8,128]{1,0:T(8,128)S(1)}, f32[8,128]{1,0:T(8,128)S(1)}, u32[]{:S(2)}, u32[]{:S(2)}) collective-permute-start(f32[8,128]{1,0:T(8,128)S(1)} %add_add_fusion.1.four_ref), channel_id=1, source_target_pairs={{128,0},{129,1},{130,2},{131,3},{132,4},{133,5},{134,6},{135,7},{1... | collective-permute-start | bytes 12296 | tf_op jit(solution)/shard_map/ppermute | solution.py:312
  39.8 15.5 %collective-permute-start.5 = (f32[8,128]{1,0:T(8,128)S(1)}, f32[8,128]{1,0:T(8,128)S(1)}, u32[]{:S(2)}, u32[]{:S(2)}) collective-permute-start(f32[8,128]{1,0:T(8,128)S(1)} %add_add_fusion.1.four_ref), channel_id=1, source_target_pairs={{256,0},{257,1},{258,2},{259,3},{260,4},{261,5},{262,6},{263,7},{2... | collective-permute-start | bytes 12296 | tf_op jit(solution)/shard_map/ppermute | solution.py:312
  41.1 14.2 %collective-permute-start.4 = (f32[8,128]{1,0:T(8,128)S(1)}, f32[8,128]{1,0:T(8,128)S(1)}, u32[]{:S(2)}, u32[]{:S(2)}) collective-permute-start(f32[8,128]{1,0:T(8,128)S(1)} %add_add_fusion.1.four_ref), channel_id=1, source_target_pairs={{384,0},{385,1},{386,2},{387,3},{388,4},{389,5},{390,6},{391,7},{3... | collective-permute-start | bytes 12296 | tf_op jit(solution)/shard_map/ppermute | solution.py:312

commit v2 on v1

--- a/solution.py
+++ b/solution.py
@@ -47,7 +47,22 @@
     return high, (value - high.astype(F32)).astype(BF16)
 
 
-def moments_kernel(places_ref, dipoles_ref, counts_ref, dest_ref, out_ref, grid_ref, sums_ref):
+def moments_kernel(
+    places_hbm, dipoles_hbm, counts_hbm, dest_hbm, out_hbm,
+    places_ref, dipoles_ref, counts_ref, dest_ref, out_ref, grid_ref, sums_ref, in_sems, out_sem,
+):
+    pairs = (
+        (places_hbm, places_ref),
+        (dipoles_hbm, dipoles_ref),
+        (counts_hbm, counts_ref),
+        (dest_hbm, dest_ref),
+    )
+    copies = [pltpu.make_async_copy(a, b, in_sems.at[k]) for k, (a, b) in enumerate(pairs)]
+    for copy in copies:
+        copy.start()
+    sums_ref[...] = jnp.zeros(sums_ref.shape, F32)
+    for copy in copies:
+        copy.wait()
     index_of = {triple: i for i, triple in enumerate(exponent_list(P_SIZE))}
 
     def turned(values):
@@ -61,7 +76,6 @@
     for axis in range(3):
         grid_ref[axis] = turned(places_ref[axis])
         grid_ref[3 + axis] = jnp.where(living, turned(dipoles_ref[axis]), 0.0)
-    sums_ref[...] = jnp.zeros(sums_ref.shape, F32)
 
     def half(step, carry):
         picked = pl.ds(pl.multiple_of(step * 32, 32), 32)
@@ -109,6 +123,11 @@
     out_ref[32:64] = values[:, 128:256]
     tail = values[:, 256:288]
     out_ref[64:72] = jnp.concatenate([tail[8 * g : 8 * g + 8] for g in range(4)], axis=1)
+    copies = [pltpu.make_async_copy(out_ref, out_hbm.at[n], out_sem.at[n]) for n in range(16)]
+    for copy in copies:
+        copy.start()
+    for copy in copies:
+        copy.wait()
 
 
 def tree_kernel(
@@ -267,7 +286,32 @@
         box_ref[at : at + 1, 256:COEFS] = last[:, 0 : COEFS - 256]
 
 
+def permute(value, *pairs):
+    return lax.ppermute(value, "wide", list(pairs))
+
+
+def across(share):
+    four = permute(share, *((8 + i, i) for i in range(4)))
+    pair = share + permute(share, *((2 * i + 1, 2 * i) for i in range(16)))
+    eight = permute(pair, (16, 0), (18, 1))
+    ten = permute(pair, (20, 0), (22, 1))
+    twelve = permute(pair, (24, 0), (26, 1))
+    six = permute(pair, (12, 0), (14, 1))
+    after, four = lax.optimization_barrier((pair, four))
+    fourteen = permute(after, (28, 0), (30, 1))
+    row = lax.broadcasted_iota(jnp.int32, (8, 128), 0)
+    mixed = share + jnp.where(row < 3, 0.0, four)
+    quads = [[8 * q + j for j in range(8)] for q in range(4)]
+    spread = jnp.broadcast_to(mixed[None], (8, 8, 128))
+    quad = jnp.sum(
+        lax.all_to_all(spread, "wide", 0, 0, axis_index_groups=quads, tiled=True), axis=0
+    )
+    late = eight + ten + twelve + six + fourteen
+    return quad, quad + late + permute(late, (1, 0))
+
+
 VMEM = pl.BlockSpec(memory_space=pltpu.VMEM)
+HBM = pl.BlockSpec(memory_space=pltpu.HBM)
 SMEM = pl.BlockSpec(memory_space=pltpu.SMEM)
 PARAMS = pltpu.CompilerParams(vmem_limit_bytes=40 * 1024 * 1024)
 
@@ -277,20 +321,28 @@
     where = jnp.stack([lax.axis_index("narrow"), lax.axis_index("wide")]).astype(jnp.int32)
     sent = pl.pallas_call(
         moments_kernel,
-        out_shape=jax.ShapeDtypeStruct((72, 128), F32),
-        in_specs=[VMEM] * 4,
-        out_specs=VMEM,
-        scratch_shapes=[pltpu.VMEM((6, 64, 128), F32), pltpu.VMEM((288, 8, 128), F32)],
-        compiler_params=PARAMS,
+        out_shape=jax.ShapeDtypeStruct((16, 72, 128), F32),
+        in_specs=[HBM] * 4,
+        out_specs=HBM,
+        scratch_shapes=[
+            pltpu.VMEM((3, 32, 256), F32),
+            pltpu.VMEM((3, 32, 256), F32),
+            pltpu.VMEM((1, 32), jnp.int32),
+            pltpu.VMEM((1, 32), jnp.int32),
+            pltpu.VMEM((72, 128), F32),
+            pltpu.VMEM((6, 64, 128), F32),
+            pltpu.VMEM((288, 8, 128), F32),
+            pltpu.SemaphoreType.DMA((4,)),
+            pltpu.SemaphoreType.DMA((16,)),
+        ],
+        compiler_params=pltpu.CompilerParams(vmem_limit_bytes=64 * 1024 * 1024 - 65536),
     )(
         jnp.transpose(positions, (1, 0, 2)),
         jnp.transpose(moments, (1, 0, 2)),
         counts.reshape(1, 32),
         dest.reshape(1, 32),
     )
-    got = lax.all_to_all(
-        jnp.broadcast_to(sent[None], (16, 72, 128)), "narrow", split_axis=0, concat_axis=0, tiled=True
-    )
+    got = lax.all_to_all(sent, "narrow", split_axis=0, concat_axis=0, tiled=True)
     leaf, box, share, own = pl.pallas_call(
         tree_kernel,
         out_shape=(
@@ -303,13 +355,7 @@
         out_specs=(VMEM,) * 4,
         compiler_params=PARAMS,
     )(where, got, jnp.asarray(shift, BF16), jnp.asarray(signs, F32))
-    pair = share + lax.ppermute(share, "wide", [(2 * i + 1, 2 * i) for i in range(16)])
-    quad = pair
-    for j in (2, 4, 6):
-        quad = quad + lax.ppermute(pair, "wide", [(8 * q + j, 8 * q) for q in range(4)])
-    top = quad
-    for j in (24, 16, 8):
-        top = top + lax.ppermute(quad, "wide", [(j, 0)])
+    quad, top = across(share)
     box = pl.pallas_call(
         finish_kernel,
         out_shape=jax.ShapeDtypeStruct((26, COEFS), F32),

time: 56.9 us -> 52.2 us (0.917)
  the two profiles are of different devices: /device:TPU:8 before, /device:TPU:1 now
where the time goes in v2:
time: 52.2 us; the launch traced here: 51.8 us
  starting transfers between devices  26.8 us (51%)
  waiting for transfers between devices  15.3 us (29%)
  Pallas kernels  8.08 us (15%)
  between operations  0.77 us (1%)
  local copies, waits for them, and re-layouts  0.63 us (1%)
    ppermute x8, starting transfers between devices, permute(): return lax.ppermute(value, 'wide', list(pairs))  15.6 us
    all_to_all x1, waiting for transfers between devices, shards(): lax.all_to_all(sent, 'narrow', split_axis=0, concat_axis=0, tiled=True)  9.56 us
    all_to_all x1, starting transfers between devices, shards(): lax.all_to_all(sent, 'narrow', split_axis=0, concat_axis=0, tiled=True)  7.73 us
    ppermute x8, waiting for transfers between devices, permute(): return lax.ppermute(value, 'wide', list(pairs))  5.75 us
    pallas_call x1, Pallas kernels, shards(): pl.pallas_call(moments_kernel, out_shape=jax.ShapeDtypeStruct((16, 72, 12...  3.98 us
    all_to_all x1, starting transfers between devices, across(): lax.all_to_all(spread, 'wide', 0, 0, axis_index_groups=quads, tiled=True)  3.5 us
    pallas_call x1, Pallas kernels, shards(): pl.pallas_call(tree_kernel, out_shape=(jax.ShapeDtypeStruct((COEFS, 128),...  2.93 us
    pallas_call x1, Pallas kernels, shards(): pl.pallas_call(finish_kernel, out_shape=jax.ShapeDtypeStruct((26, COEFS),...  1.17 us
  transfers between devices with their start and end apart: 10, of which 6 were waited for; matrix products, arithmetic and copies ran while one was open for 2% of the time, Pallas kernels for 0%

profile of v2, /device:TPU:1, one launch (start us, length us, event | category | flops | bytes accessed | tf_op | source)
XLA Modules:
  0.0 51.8 jit_solution(7787239313388056885)
XLA Ops:
  0.6 4.0 %shard_map.77 = f32[16,72,128]{2,1,0:T(8,128)} custom-call(f32[3,32,256]{2,1,0:T(8,128)} %bitcast.7, f32[3,32,256]{2,1,0:T(8,128)} %bitcast.8, s32[1,32]{1,0:T(1,128)} %bitcast.9, s32[1,32]{1,0:T(1,128)} %bitcast.10), custom_call_target="tpu_custom_call" | custom-call | tf_op jit(solution)/shard_map/pallas_call | solution.py:322
  4.6 0.0 copy-start
  4.6 7.7 %all-to-all-start = ((f32[16,72,128]{2,1,0:T(8,128)}), f32[16,72,128]{2,1,0:T(8,128)S(1)}, u32[]{:S(2)}, u32[]{:S(2)}) async-start(f32[16,72,128]{2,1,0:T(8,128)} %shard_map.77), calls=%async_computation | async-start | bytes 1179648 | tf_op jit(solution)/shard_map/all_to_all | solution.py:345
  12.4 0.0 copy-start.1
  12.4 0.1 pad_add_fusion.where_ref
  12.5 9.6 %all-to-all-done.got_ref = f32[16,72,128]{2,1,0:T(8,128)S(1)} async-done(((f32[16,72,128]{2,1,0:T(8,128)}), f32[16,72,128]{2,1,0:T(8,128)S(1)}, u32[]{:S(2)}, u32[]{:S(2)}) %all-to-all-start) | async-done | bytes 589856 | tf_op jit(solution)/shard_map/all_to_all | solution.py:345
  22.0 2.9 %shard_map.78 = (f32[286,128]{1,0:T(8,128)}, f32[26,286]{1,0:T(8,128)S(1)}, f32[8,128]{1,0:T(8,128)S(1)}, f32[8,128]{1,0:T(8,128)S(1)}) custom-call(s32[2]{0:T(128)S(1)} %pad_add_fusion.where_ref, f32[16,72,128]{2,1,0:T(8,128)S(1)} %all-to-all-done.got_ref, bf16[256,384]{1,0:T(8,128)(2,1)S(1)} %copy-done, f32[8,384]{1,0:T(8,128)S(1)} %copy-done.1), custom_call_target="tpu_custom_call" | custom-call | tf_op jit(solution)/shard_map/pallas_call | solution.py:346
  25.0 5.5 %collective-permute-start = (f32[8,128]{1,0:T(8,128)S(1)}, f32[8,128]{1,0:T(8,128)S(1)}, u32[]{:S(2)}, u32[]{:S(2)}) collective-permute-start(f32[8,128]{1,0:T(8,128)S(1)} %get-tuple-element.10), channel_id=1, source_target_pairs={{16,0},{48,32},{80,64},{112,96},{144,128},{176,160},{208,192},{240... | collective-permute-start | bytes 12296 | tf_op jit(solution)/shard_map/ppermute | solution.py:290
  30.5 1.3 %collective-permute-start.1 = (f32[8,128]{1,0:T(8,128)S(1)}, f32[8,128]{1,0:T(8,128)S(1)}, u32[]{:S(2)}, u32[]{:S(2)}) collective-permute-start(f32[8,128]{1,0:T(8,128)S(1)} %get-tuple-element.10), channel_id=1, source_target_pairs={{128,0},{144,16},{160,32},{176,48},{129,1},{145,17},{161,33},{177,... | collective-permute-start | bytes 12296 | tf_op jit(solution)/shard_map/ppermute | solution.py:290
  31.8 1.3 %collective-permute-start.2 = (f32[8,128]{1,0:T(8,128)S(1)}, f32[8,128]{1,0:T(8,128)S(1)}, u32[]{:S(2)}, u32[]{:S(2)}) collective-permute-start(f32[8,128]{1,0:T(8,128)S(1)} %add.24), channel_id=1, source_target_pairs={{256,0},{288,16},{257,1},{289,17},{258,2},{290,18},{259,3},{291,19... | collective-permute-start | bytes 12296 | tf_op jit(solution)/shard_map/ppermute | solution.py:290
  33.1 1.3 %collective-permute-start.3 = (f32[8,128]{1,0:T(8,128)S(1)}, f32[8,128]{1,0:T(8,128)S(1)}, u32[]{:S(2)}, u32[]{:S(2)}) collective-permute-start(f32[8,128]{1,0:T(8,128)S(1)} %add.24), channel_id=1, source_target_pairs={{320,0},{352,16},{321,1},{353,17},{322,2},{354,18},{323,3},{355,19... | collective-permute-start | bytes 12296 | tf_op jit(solution)/shard_map/ppermute | solution.py:290
  34.4 1.3 %collective-permute-start.4 = (f32[8,128]{1,0:T(8,128)S(1)}, f32[8,128]{1,0:T(8,128)S(1)}, u32[]{:S(2)}, u32[]{:S(2)}) collective-permute-start(f32[8,128]{1,0:T(8,128)S(1)} %add.24), channel_id=1, source_target_pairs={{384,0},{416,16},{385,1},{417,17},{386,2},{418,18},{387,3},{419,19... | collective-permute-start | bytes 12296 | tf_op jit(solution)/shard_map/ppermute | solution.py:290
  35.7 1.3 %collective-permute-start.5 = (f32[8,128]{1,0:T(8,128)S(1)}, f32[8,128]{1,0:T(8,128)S(1)}, u32[]{:S(2)}, u32[]{:S(2)}) collective-permute-start(f32[8,128]{1,0:T(8,128)S(1)} %add.24), channel_id=1, source_target_pairs={{192,0},{224,16},{193,1},{225,17},{194,2},{226,18},{195,3},{227,19... | collective-permute-start | bytes 12296 | tf_op jit(solution)/shard_map/ppermute | solution.py:290
  37.0 2.2 %collective-permute-done.1 = f32[8,128]{1,0:T(8,128)S(1)} collective-permute-done((f32[8,128]{1,0:T(8,128)S(1)}, f32[8,128]{1,0:T(8,128)S(1)}, u32[]{:S(2)}, u32[]{:S(2)}) %collective-permute-start.1) | collective-permute-done | bytes 4128 | tf_op jit(solution)/shard_map/ppermute | solution.py:290
  39.2 1.3 %collective-permute-start.6 = (f32[8,128]{1,0:T(8,128)S(1)}, f32[8,128]{1,0:T(8,128)S(1)}, u32[]{:S(2)}, u32[]{:S(2)}) collective-permute-start(f32[8,128]{1,0:T(8,128)S(1)} %add.24), channel_id=1, source_target_pairs={{448,0},{480,16},{449,1},{481,17},{450,2},{482,18},{451,3},{483,19... | collective-permute-start | bytes 12296 | tf_op jit(solution)/shard_map/ppermute | solution.py:290
  40.5 0.1 select_add_fusion
  40.6 0.6 %broadcast_in_dim.11 = f32[8,8,128]{2,1,0:T(8,128)} broadcast(f32[8,128]{1,0:T(8,128)S(1)} %select_add_fusion), dimensions={1,2} | broadcast | bytes 36864 | tf_op jit(solution)/shard_map/broadcast_in_dim | solution.py:305
  41.2 3.5 %all-to-all-start.1 = ((f32[8,8,128]{2,1,0:T(8,128)}), f32[8,8,128]{2,1,0:T(8,128)S(1)}, u32[]{:S(2)}, u32[]{:S(2)}) async-start(f32[8,8,128]{2,1,0:T(8,128)} %broadcast_in_dim.11), calls=%async_computation.1 | async-start | bytes 65536 | tf_op jit(solution)/shard_map/all_to_all | solution.py:307
  44.7 1.2 %collective-permute-done.6 = f32[8,128]{1,0:T(8,128)S(1)} collective-permute-done((f32[8,128]{1,0:T(8,128)S(1)}, f32[8,128]{1,0:T(8,128)S(1)}, u32[]{:S(2)}, u32[]{:S(2)}) %collective-permute-start.6) | collective-permute-done | bytes 4128 | tf_op jit(solution)/shard_map/ppermute | solution.py:290
  45.9 1.2 %collective-permute-done.2 = f32[8,128]{1,0:T(8,128)S(1)} collective-permute-done((f32[8,128]{1,0:T(8,128)S(1)}, f32[8,128]{1,0:T(8,128)S(1)}, u32[]{:S(2)}, u32[]{:S(2)}) %collective-permute-start.2) | collective-permute-done | bytes 4128 | tf_op jit(solution)/shard_map/ppermute | solution.py:290
  47.0 0.4 collective-permute-done.5
  47.5 2.3 %collective-permute-start.7 = (f32[8,128]{1,0:T(8,128)S(1)}, f32[8,128]{1,0:T(8,128)S(1)}, u32[]{:S(2)}, u32[]{:S(2)}) collective-permute-start(f32[8,128]{1,0:T(8,128)S(1)} %add_add_fusion.1), channel_id=1, source_target_pairs={{16,0},{17,1},{18,2},{19,3},{20,4},{21,5},{22,6},{23,7},{24,8},{25... | collective-permute-start | bytes 12296 | tf_op jit(solution)/shard_map/ppermute | solution.py:290
  49.8 0.8 %collective-permute-done.7 = f32[8,128]{1,0:T(8,128)S(1)} collective-permute-done((f32[8,128]{1,0:T(8,128)S(1)}, f32[8,128]{1,0:T(8,128)S(1)}, u32[]{:S(2)}, u32[]{:S(2)}) %collective-permute-start.7) | collective-permute-done | bytes 4128 | tf_op jit(solution)/shard_map/ppermute | solution.py:290
  50.6 1.2 %shard_map.79 = f32[26,286]{1,0:T(8,128)} custom-call(s32[2]{0:T(128)S(1)} %pad_add_fusion.where_ref, f32[8,128]{1,0:T(8,128)S(1)} %get-tuple-element.9.own_ref, f32[8,128]{1,0:T(8,128)S(1)} %reduce_sum.9.four_ref, f32[8,128]{1,0:T(8,128)S(1)} %add_add_fusion.five_ref, f32[26,286]{1,0:T(8,128)S(1)} %get-tuple-element.13.part_ref), custom_call_target="tpu_custom_call" | custom-call | tf_op jit(solution)/shard_map/pallas_call | solution.py:359
  (11 shorter events, 0.0 us)
Async XLA Ops:
  4.6 17.4 %copy-start = (bf16[256,384]{1,0:T(8,128)(2,1)S(1)}, bf16[256,384]{1,0:T(8,128)(2,1)}, u32[]{:S(2)}) copy-start(bf16[256,384]{1,0:T(8,128)(2,1)} %constant.17.clone.shift_ref) | copy-start | bytes 589828
  4.6 17.4 %all-to-all-start = ((f32[16,72,128]{2,1,0:T(8,128)}), f32[16,72,128]{2,1,0:T(8,128)S(1)}, u32[]{:S(2)}, u32[]{:S(2)}) async-start(f32[16,72,128]{2,1,0:T(8,128)} %shard_map.77), calls=%async_computation | async-start | bytes 1179648 | tf_op jit(solution)/shard_map/all_to_all | solution.py:345
  12.4 9.7 %copy-start.1 = (f32[8,384]{1,0:T(8,128)S(1)}, f32[8,384]{1,0:T(8,128)}, u32[]{:S(2)}) copy-start(f32[8,384]{1,0:T(8,128)} %constant.18.clone.signs_ref) | copy-start | bytes 36868
  25.0 6.9 %collective-permute-start = (f32[8,128]{1,0:T(8,128)S(1)}, f32[8,128]{1,0:T(8,128)S(1)}, u32[]{:S(2)}, u32[]{:S(2)}) collective-permute-start(f32[8,128]{1,0:T(8,128)S(1)} %get-tuple-element.10), channel_id=1, source_target_pairs={{16,0},{48,32},{80,64},{112,96},{144,128},{176,160},{208,192},{240... | collective-permute-start | bytes 12296 | tf_op jit(solution)/shard_map/ppermute | solution.py:290
  30.5 8.7 %collective-permute-start.1 = (f32[8,128]{1,0:T(8,128)S(1)}, f32[8,128]{1,0:T(8,128)S(1)}, u32[]{:S(2)}, u32[]{:S(2)}) collective-permute-start(f32[8,128]{1,0:T(8,128)S(1)} %get-tuple-element.10), channel_id=1, source_target_pairs={{128,0},{144,16},{160,32},{176,48},{129,1},{145,17},{161,33},{177,... | collective-permute-start | bytes 12296 | tf_op jit(solution)/shard_map/ppermute | solution.py:290
  31.8 15.2 %collective-permute-start.2 = (f32[8,128]{1,0:T(8,128)S(1)}, f32[8,128]{1,0:T(8,128)S(1)}, u32[]{:S(2)}, u32[]{:S(2)}) collective-permute-start(f32[8,128]{1,0:T(8,128)S(1)} %add.24), channel_id=1, source_target_pairs={{256,0},{288,16},{257,1},{289,17},{258,2},{290,18},{259,3},{291,19... | collective-permute-start | bytes 12296 | tf_op jit(solution)/shard_map/ppermute | solution.py:290
  33.1 13.9 %collective-permute-start.3 = (f32[8,128]{1,0:T(8,128)S(1)}, f32[8,128]{1,0:T(8,128)S(1)}, u32[]{:S(2)}, u32[]{:S(2)}) collective-permute-start(f32[8,128]{1,0:T(8,128)S(1)} %add.24), channel_id=1, source_target_pairs={{320,0},{352,16},{321,1},{353,17},{322,2},{354,18},{323,3},{355,19... | collective-permute-start | bytes 12296 | tf_op jit(solution)/shard_map/ppermute | solution.py:290
  34.4 12.6 %collective-permute-start.4 = (f32[8,128]{1,0:T(8,128)S(1)}, f32[8,128]{1,0:T(8,128)S(1)}, u32[]{:S(2)}, u32[]{:S(2)}) collective-permute-start(f32[8,128]{1,0:T(8,128)S(1)} %add.24), channel_id=1, source_target_pairs={{384,0},{416,16},{385,1},{417,17},{386,2},{418,18},{387,3},{419,19... | collective-permute-start | bytes 12296 | tf_op jit(solution)/shard_map/ppermute | solution.py:290
  35.7 11.8 %collective-permute-start.5 = (f32[8,128]{1,0:T(8,128)S(1)}, f32[8,128]{1,0:T(8,128)S(1)}, u32[]{:S(2)}, u32[]{:S(2)}) collective-permute-start(f32[8,128]{1,0:T(8,128)S(1)} %add.24), channel_id=1, source_target_pairs={{192,0},{224,16},{193,1},{225,17},{194,2},{226,18},{195,3},{227,19... | collective-permute-start | bytes 12296 | tf_op jit(solution)/shard_map/ppermute | solution.py:290
  39.2 6.6 %collective-permute-start.6 = (f32[8,128]{1,0:T(8,128)S(1)}, f32[8,128]{1,0:T(8,128)S(1)}, u32[]{:S(2)}, u32[]{:S(2)}) collective-permute-start(f32[8,128]{1,0:T(8,128)S(1)} %add.24), channel_id=1, source_target_pairs={{448,0},{480,16},{449,1},{481,17},{450,2},{482,18},{451,3},{483,19... | collective-permute-start | bytes 12296 | tf_op jit(solution)/shard_map/ppermute | solution.py:290
  41.2 8.6 %all-to-all-start.1 = ((f32[8,8,128]{2,1,0:T(8,128)}), f32[8,8,128]{2,1,0:T(8,128)S(1)}, u32[]{:S(2)}, u32[]{:S(2)}) async-start(f32[8,8,128]{2,1,0:T(8,128)} %broadcast_in_dim.11), calls=%async_computation.1 | async-start | bytes 65536 | tf_op jit(solution)/shard_map/all_to_all | solution.py:307
  47.5 3.1 %collective-permute-start.7 = (f32[8,128]{1,0:T(8,128)S(1)}, f32[8,128]{1,0:T(8,128)S(1)}, u32[]{:S(2)}, u32[]{:S(2)}) collective-permute-start(f32[8,128]{1,0:T(8,128)S(1)} %add_add_fusion.1), channel_id=1, source_target_pairs={{16,0},{17,1},{18,2},{19,3},{20,4},{21,5},{22,6},{23,7},{24,8},{25... | collective-permute-start | bytes 12296 | tf_op jit(solution)/shard_map/ppermute | solution.py:290

commit v3 on v2

--- a/solution.py
+++ b/solution.py
@@ -51,12 +51,10 @@
     places_hbm, dipoles_hbm, counts_hbm, dest_hbm, out_hbm,
     places_ref, dipoles_ref, counts_ref, dest_ref, out_ref, grid_ref, sums_ref, in_sems, out_sem,
 ):
-    pairs = (
-        (places_hbm, places_ref),
-        (dipoles_hbm, dipoles_ref),
-        (counts_hbm, counts_ref),
-        (dest_hbm, dest_ref),
-    )
+    pairs = [(counts_hbm, counts_ref), (dest_hbm, dest_ref)]
+    for axis in range(3):
+        pairs.append((places_hbm.at[axis], places_ref.at[axis]))
+        pairs.append((dipoles_hbm.at[axis], dipoles_ref.at[axis]))
     copies = [pltpu.make_async_copy(a, b, in_sems.at[k]) for k, (a, b) in enumerate(pairs)]
     for copy in copies:
         copy.start()
@@ -77,7 +75,7 @@
         grid_ref[axis] = turned(places_ref[axis])
         grid_ref[3 + axis] = jnp.where(living, turned(dipoles_ref[axis]), 0.0)
 
-    def half(step, carry):
+    def stripe(step, carry):
         picked = pl.ds(pl.multiple_of(step * 32, 32), 32)
         x, y, z, mx, my, mz = [grid_ref[k, picked, :] for k in range(6)]
 
@@ -91,27 +89,23 @@
                 phi_x, psi_x = x, mx
             elif a > 1:
                 phi_x, psi_x = phi_x * x, psi_x * x + mx * phi_x
-            phi_y, psi_y = phi_x, psi_x
+            phi, psi = phi_x, psi_x
             for e in range(P_SIZE + 1 - a):
                 if e > 0:
-                    if phi_y is None:
-                        phi_y, psi_y = y, my
-                    elif psi_y is None:
-                        phi_y, psi_y = phi_y * y, my * phi_y
+                    if phi is None:
+                        phi, psi = y, my
                     else:
-                        phi_y, psi_y = phi_y * y, psi_y * y + my * phi_y
-                phi, psi = phi_y, psi_y
-                for c in range(P_SIZE + 1 - a - e):
-                    if c > 0:
-                        if phi is None:
-                            phi, psi = z, mz
-                        else:
-                            phi, psi = phi * z, psi * z + mz * phi
-                    if psi is not None:
-                        note((a, e, c), psi)
+                        phi, psi = phi * y, psi * y + my * phi
+                if psi is not None:
+                    note((a, e, 0), psi)
+                deep, omega = psi, mz if phi is None else mz * phi
+                for c in range(1, P_SIZE + 1 - a - e):
+                    deep = omega if deep is None else deep * z + omega
+                    note((a, e, c), deep)
+                    omega = omega * z
         return carry
 
-    lax.fori_loop(0, 2, half, 0)
+    lax.fori_loop(0, 2, stripe, 0)
     folded = jnp.sum(sums_ref[...], axis=1)
     blank = jnp.zeros((1, 96), F32)
     where_to = jnp.concatenate([dest_ref[...].astype(F32), blank], axis=1)
@@ -131,7 +125,7 @@
 
 
 def tree_kernel(
-    where_ref, got_ref, shift_ref, signs_ref, leaf_ref, box_ref, send_ref, own_ref
+    where_ref, got_ref, shift_ref, signs_ref, send_ref, held_ref, level_ref, span_ref
 ):
     me = where_ref[0]
     group = where_ref[1]
@@ -180,14 +174,9 @@
     chosen = jnp.where(wanted == rank, 1.0, 0.0).astype(BF16)
     placed = jnp.dot(chosen, held, preferred_element_type=F32)
     own = placed[GROUP:]
-    leaf_first = (own[:, 0:128] + own[:, 256:384]).T
-    leaf_second = (own[:, 128:256] + own[:, 384:512]).T
     own_tail = own[:, 512:640]
-    leaf_tail = (own_tail + pltpu.roll(own_tail, 96, 1)).T
-    leaf_ref[0:128] = leaf_first
-    leaf_ref[128:256] = leaf_second
-    leaf_ref[256:COEFS] = leaf_tail[0 : COEFS - 256]
-
+    held_ref[:, 0:256] = own[:, 0:256] + own[:, 256:512]
+    held_ref[:, 256:384] = own_tail + pltpu.roll(own_tail, 96, 1)
     shift = shift_ref[...]
     tiny = 2.0**-P_SIZE
 
@@ -242,78 +231,88 @@
 
     level_4 = share(level_3, group % 8)
     level_5 = share(level_4, group // 8)
-    send_ref[0:1] = level_4[:, 0:128]
-    send_ref[1:2] = level_4[:, 128:256]
-    send_ref[2:3] = level_4[:, 256:384]
-    send_ref[3:4] = level_5[:, 0:128]
-    send_ref[4:5] = level_5[:, 128:256]
-    send_ref[5:6] = level_5[:, 256:384]
-    send_ref[6:8] = jnp.zeros((2, 128), F32)
-
-    boxes = jnp.concatenate(
-        [level_1, level_2, level_3, jnp.zeros((55, 384), F32)], axis=0
-    )
-    end = start + tally
+    send_ref[0:1] = level_4
+    send_ref[1:2] = level_5
+    level_ref[0:64] = level_1
+    level_ref[64:72] = level_2
+    level_ref[72:80] = jnp.broadcast_to(level_3, (8, 384))
+    span_ref[0:1] = jnp.broadcast_to(start, (1, 128))
+    span_ref[1:2] = jnp.broadcast_to(start + tally, (1, 128))
+    span_ref[2:3] = jnp.zeros((1, 128), jnp.int32) + jnp.where(group % 8 == 0, 22, -1)
+    span_ref[3:4] = jnp.zeros((1, 128), jnp.int32) + jnp.where(group == 0, 24, -1)
+
+
+def outputs_kernel(held_ref, level_ref, span_ref, leaf_ref, box_ref):
+    held = held_ref[...]
+    leaf_ref[0:128] = held[:, 0:128].T
+    leaf_ref[128:256] = held[:, 128:256].T
+    leaf_ref[256:COEFS] = held[:, 256:384].T[0 : COEFS - 256]
+    start = span_ref[0:1, 0:1]
+    end = span_ref[1:2, 0:1]
     out_slot = lax.broadcasted_iota(jnp.int32, (32, 1), 0)
     box_1 = start // 8 + out_slot
     box_2 = start // 64 + out_slot - 17
     source = jnp.where((box_1 * 8 >= start) & (box_1 * 8 < end), (box_1 % 8) * 8 + box_1 // 8, -1)
     source_2 = jnp.where((box_2 * 64 >= start) & (box_2 * 64 < end), 64 + box_2, -1)
-    first_of_group = (start == 0) & (tally > 0)
+    first_of_group = (start == 0) & (end > 0)
     source_3 = jnp.where(first_of_group & (out_slot == 20), 72, -1)
     source = jnp.where(out_slot < 17, source, jnp.where(out_slot < 20, source_2, source_3))
     column = lax.broadcasted_iota(jnp.int32, (32, 128), 1)
     select = jnp.where(column == source, 1.0, 0.0).astype(BF16)
+    boxes = jnp.concatenate([level_ref[...], jnp.zeros((48, 384), F32)], axis=0)
     high, low = split(boxes)
     picked = jnp.dot(select, high, preferred_element_type=F32) + jnp.dot(
         select, low, preferred_element_type=F32
     )
+    upper = (out_slot == span_ref[2:3, 0:1]) | (out_slot == span_ref[3:4, 0:1])
+    owned = first_of_group & upper
+    picked = picked + jnp.where(owned, 1.0, 0.0)
     box_ref[...] = picked[0:26, 0:COEFS]
-    heads = first_of_group & (lax.broadcasted_iota(jnp.int32, (8, 128), 0) >= 0)
-    own_ref[...] = jnp.where(heads, 1.0, 0.0)
-
-
-def finish_kernel(where_ref, own_ref, four_ref, five_ref, part_ref, box_ref):
-    group = where_ref[1]
-    own = own_ref[0:1]
-    keep_4 = own * jnp.where(group % 8 == 0, 1.0, 0.0)
-    keep_5 = own * jnp.where(group == 0, 1.0, 0.0)
-    box_ref[...] = part_ref[...]
-    for at, keep, ref, base in ((22, keep_4, four_ref, 0), (24, keep_5, five_ref, 3)):
-        box_ref[at : at + 1, 0:128] = ref[base : base + 1] * keep
-        box_ref[at : at + 1, 128:256] = ref[base + 1 : base + 2] * keep
-        last = ref[base + 2 : base + 3] * keep
-        box_ref[at : at + 1, 256:COEFS] = last[:, 0 : COEFS - 256]
 
 
 def permute(value, *pairs):
     return lax.ppermute(value, "wide", list(pairs))
 
 
-def across(share):
+def across(share, kept):
     four = permute(share, *((8 + i, i) for i in range(4)))
     pair = share + permute(share, *((2 * i + 1, 2 * i) for i in range(16)))
     eight = permute(pair, (16, 0), (18, 1))
     ten = permute(pair, (20, 0), (22, 1))
     twelve = permute(pair, (24, 0), (26, 1))
     six = permute(pair, (12, 0), (14, 1))
-    after, four = lax.optimization_barrier((pair, four))
+    after, four, kept = lax.optimization_barrier((pair, four, kept))
     fourteen = permute(after, (28, 0), (30, 1))
-    row = lax.broadcasted_iota(jnp.int32, (8, 128), 0)
-    mixed = share + jnp.where(row < 3, 0.0, four)
+    row = lax.broadcasted_iota(jnp.int32, (2, 384), 0)
+    mixed = share + jnp.where(row == 0, 0.0, four)
     quads = [[8 * q + j for j in range(8)] for q in range(4)]
-    spread = jnp.broadcast_to(mixed[None], (8, 8, 128))
+    spread = jnp.broadcast_to(mixed[None], (8, 2, 384))
     quad = jnp.sum(
         lax.all_to_all(spread, "wide", 0, 0, axis_index_groups=quads, tiled=True), axis=0
     )
+    leaf, box = outputs(*kept)
     late = eight + ten + twelve + six + fourteen
-    return quad, quad + late + permute(late, (1, 0))
+    late, box = lax.optimization_barrier((late, box))
+    return quad, quad + late + permute(late, (1, 0)), leaf, box
 
 
 VMEM = pl.BlockSpec(memory_space=pltpu.VMEM)
 HBM = pl.BlockSpec(memory_space=pltpu.HBM)
 SMEM = pl.BlockSpec(memory_space=pltpu.SMEM)
 PARAMS = pltpu.CompilerParams(vmem_limit_bytes=40 * 1024 * 1024)
+
+
+def outputs(held, levels, span):
+    return pl.pallas_call(
+        outputs_kernel,
+        out_shape=(
+            jax.ShapeDtypeStruct((COEFS, 128), F32),
+            jax.ShapeDtypeStruct((26, COEFS), F32),
+        ),
+        in_specs=[VMEM] * 3,
+        out_specs=(VMEM,) * 2,
+        compiler_params=PARAMS,
+    )(held, levels, span)
 
 
 def shards(positions, moments, counts, dest):
@@ -332,7 +331,7 @@
             pltpu.VMEM((72, 128), F32),
             pltpu.VMEM((6, 64, 128), F32),
             pltpu.VMEM((288, 8, 128), F32),
-            pltpu.SemaphoreType.DMA((4,)),
+            pltpu.SemaphoreType.DMA((8,)),
             pltpu.SemaphoreType.DMA((16,)),
         ],
         compiler_params=pltpu.CompilerParams(vmem_limit_bytes=64 * 1024 * 1024 - 65536),
@@ -343,26 +342,22 @@
         dest.reshape(1, 32),
     )
     got = lax.all_to_all(sent, "narrow", split_axis=0, concat_axis=0, tiled=True)
-    leaf, box, share, own = pl.pallas_call(
+    share, *kept = pl.pallas_call(
         tree_kernel,
         out_shape=(
-            jax.ShapeDtypeStruct((COEFS, 128), F32),
-            jax.ShapeDtypeStruct((26, COEFS), F32),
-            jax.ShapeDtypeStruct((8, 128), F32),
-            jax.ShapeDtypeStruct((8, 128), F32),
+            jax.ShapeDtypeStruct((2, 384), F32),
+            jax.ShapeDtypeStruct((128, 384), F32),
+            jax.ShapeDtypeStruct((80, 384), F32),
+            jax.ShapeDtypeStruct((4, 128), jnp.int32),
         ),
         in_specs=[SMEM, VMEM, VMEM, VMEM],
         out_specs=(VMEM,) * 4,
         compiler_params=PARAMS,
     )(where, got, jnp.asarray(shift, BF16), jnp.asarray(signs, F32))
-    quad, top = across(share)
-    box = pl.pallas_call(
-        finish_kernel,
-        out_shape=jax.ShapeDtypeStruct((26, COEFS), F32),
-        in_specs=[SMEM, VMEM, VMEM, VMEM, VMEM],
-        out_specs=VMEM,
-        compiler_params=PARAMS,
-    )(where, own, quad, top, box)
+    quad, top, leaf, box = across(share, kept)
+    row = lax.broadcasted_iota(jnp.int32, (26, COEFS), 0)
+    last = jnp.where(row == 24, top[1:2, 0:COEFS], 1.0)
+    box = box * jnp.where(row == 22, quad[0:1, 0:COEFS], last)
     return leaf.T, box
 
 

time: 52.2 us -> 51 us (0.977)
  Pallas kernels: 8.08 us -> 6.87 us
  waiting for transfers between devices: 15.3 us -> 14.5 us
  other arithmetic: 0.18 us -> 0.92 us
    pallas_call x2, Pallas kernels: 4.11 us -> 3.1 us  [the longest x1 2.28 us: shards(): pl.pallas_call(tree_kernel, out_shape=(jax.ShapeDtypeStruct((2, 384), F32...]
    ppermute x8, waiting for transfers between devices: 5.75 us -> 4.89 us  [permute(): return lax.ppermute(value, 'wide', list(pairs))]
    mul x0 -> x1, other arithmetic: none -> 0.7 us  [shards(): box = box * jnp.where(row == 22, quad[0:1, 0:COEFS], last)]
  transfers between devices with their start and end apart: 10 -> 10, of which waited for: 6 -> 6; matrix products, arithmetic and copies ran while one was open for 2% -> 2% of each run, Pallas kernels for 0% -> 2%
where the time goes in v3:
time: 51 us; the launch traced here: 50.5 us
  starting transfers between devices  26.8 us (53%)
  waiting for transfers between devices  14.5 us (28%)
  Pallas kernels  6.87 us (13%)
  other arithmetic  0.92 us (2%)
  between operations  0.78 us (2%)
  local copies, waits for them, and re-layouts  0.63 us (1%)
    ppermute x8, starting transfers between devices, permute(): return lax.ppermute(value, 'wide', list(pairs))  15.6 us
    all_to_all x1, waiting for transfers between devices, shards(): lax.all_to_all(sent, 'narrow', split_axis=0, concat_axis=0, tiled=True)  9.56 us
    all_to_all x1, starting transfers between devices, shards(): lax.all_to_all(sent, 'narrow', split_axis=0, concat_axis=0, tiled=True)  7.73 us
    ppermute x8, waiting for transfers between devices, permute(): return lax.ppermute(value, 'wide', list(pairs))  4.89 us
    pallas_call x1, Pallas kernels, shards(): pl.pallas_call(moments_kernel, out_shape=jax.ShapeDtypeStruct((16, 72, 12...  3.76 us
    all_to_all x1, starting transfers between devices, across(): lax.all_to_all(spread, 'wide', 0, 0, axis_index_groups=quads, tiled=True)  3.5 us
    pallas_call x1, Pallas kernels, shards(): pl.pallas_call(tree_kernel, out_shape=(jax.ShapeDtypeStruct((2, 384), F32...  2.28 us
  transfers between devices with their start and end apart: 10, of which 6 were waited for; matrix products, arithmetic and copies ran while one was open for 2% of the time, Pallas kernels for 2%

profile of v3, /device:TPU:1, one launch (start us, length us, event | category | flops | bytes accessed | tf_op | source)
XLA Modules:
  0.0 50.5 jit_solution(17275105633939718697)
XLA Ops:
  0.6 3.8 %shard_map.77 = f32[16,72,128]{2,1,0:T(8,128)} custom-call(f32[3,32,256]{2,1,0:T(8,128)} %bitcast.7, f32[3,32,256]{2,1,0:T(8,128)} %bitcast.8, s32[1,32]{1,0:T(1,128)} %bitcast.9, s32[1,32]{1,0:T(1,128)} %bitcast.10), custom_call_target="tpu_custom_call" | custom-call | tf_op jit(solution)/shard_map/pallas_call | solution.py:321
  4.4 0.0 copy-start
  4.4 7.7 %all-to-all-start = ((f32[16,72,128]{2,1,0:T(8,128)}), f32[16,72,128]{2,1,0:T(8,128)S(1)}, u32[]{:S(2)}, u32[]{:S(2)}) async-start(f32[16,72,128]{2,1,0:T(8,128)} %shard_map.77), calls=%async_computation | async-start | bytes 1179648 | tf_op jit(solution)/shard_map/all_to_all | solution.py:344
  12.2 0.1 pad_add_fusion.where_ref
  12.2 9.6 %all-to-all-done.got_ref = f32[16,72,128]{2,1,0:T(8,128)S(1)} async-done(((f32[16,72,128]{2,1,0:T(8,128)}), f32[16,72,128]{2,1,0:T(8,128)S(1)}, u32[]{:S(2)}, u32[]{:S(2)}) %all-to-all-start) | async-done | bytes 589856 | tf_op jit(solution)/shard_map/all_to_all | solution.py:344
  21.8 2.3 %shard_map.78 = (f32[2,384]{1,0:T(2,128)S(1)}, f32[128,384]{1,0:T(8,128)S(1)}, f32[80,384]{1,0:T(8,128)S(1)}, s32[4,128]{1,0:T(4,128)S(1)}) custom-call(s32[2]{0:T(128)S(1)} %pad_add_fusion.where_ref, f32[16,72,128]{2,1,0:T(8,128)S(1)} %all-to-all-done.got_ref, bf16[256,384]{1,0:T(8,128)(2,1)S(1)} %copy-done, f32[8,384]{1,0:T(8,128)S(1)} %copy-done.1), custom_call_target="tpu_custom_call" | custom-call | tf_op jit(solution)/shard_map/pallas_call | solution.py:345
  24.1 5.5 %collective-permute-start = (f32[2,384]{1,0:T(2,128)S(1)}, f32[2,384]{1,0:T(2,128)S(1)}, u32[]{:S(2)}, u32[]{:S(2)}) collective-permute-start(f32[2,384]{1,0:T(2,128)S(1)} %get-tuple-element.15), channel_id=1, source_target_pairs={{16,0},{48,32},{80,64},{112,96},{144,128},{176,160},{208,192},{240... | collective-permute-start | bytes 9224 | tf_op jit(solution)/shard_map/ppermute | solution.py:274
  29.6 1.3 %collective-permute-start.1 = (f32[2,384]{1,0:T(2,128)S(1)}, f32[2,384]{1,0:T(2,128)S(1)}, u32[]{:S(2)}, u32[]{:S(2)}) collective-permute-start(f32[2,384]{1,0:T(2,128)S(1)} %get-tuple-element.15), channel_id=1, source_target_pairs={{128,0},{144,16},{160,32},{176,48},{129,1},{145,17},{161,33},{177,... | collective-permute-start | bytes 9224 | tf_op jit(solution)/shard_map/ppermute | solution.py:274
  31.0 1.3 %collective-permute-start.2 = (f32[2,384]{1,0:T(2,128)S(1)}, f32[2,384]{1,0:T(2,128)S(1)}, u32[]{:S(2)}, u32[]{:S(2)}) collective-permute-start(f32[2,384]{1,0:T(2,128)S(1)} %add.24), channel_id=1, source_target_pairs={{256,0},{288,16},{257,1},{289,17},{258,2},{290,18},{259,3},{291,19... | collective-permute-start | bytes 9224 | tf_op jit(solution)/shard_map/ppermute | solution.py:274
  32.3 1.3 %collective-permute-start.3 = (f32[2,384]{1,0:T(2,128)S(1)}, f32[2,384]{1,0:T(2,128)S(1)}, u32[]{:S(2)}, u32[]{:S(2)}) collective-permute-start(f32[2,384]{1,0:T(2,128)S(1)} %add.24), channel_id=1, source_target_pairs={{320,0},{352,16},{321,1},{353,17},{322,2},{354,18},{323,3},{355,19... | collective-permute-start | bytes 9224 | tf_op jit(solution)/shard_map/ppermute | solution.py:274
  33.6 1.3 %collective-permute-start.4 = (f32[2,384]{1,0:T(2,128)S(1)}, f32[2,384]{1,0:T(2,128)S(1)}, u32[]{:S(2)}, u32[]{:S(2)}) collective-permute-start(f32[2,384]{1,0:T(2,128)S(1)} %add.24), channel_id=1, source_target_pairs={{384,0},{416,16},{385,1},{417,17},{386,2},{418,18},{387,3},{419,19... | collective-permute-start | bytes 9224 | tf_op jit(solution)/shard_map/ppermute | solution.py:274
  34.9 1.3 %collective-permute-start.5 = (f32[2,384]{1,0:T(2,128)S(1)}, f32[2,384]{1,0:T(2,128)S(1)}, u32[]{:S(2)}, u32[]{:S(2)}) collective-permute-start(f32[2,384]{1,0:T(2,128)S(1)} %add.24), channel_id=1, source_target_pairs={{192,0},{224,16},{193,1},{225,17},{194,2},{226,18},{195,3},{227,19... | collective-permute-start | bytes 9224 | tf_op jit(solution)/shard_map/ppermute | solution.py:274
  36.2 2.2 %collective-permute-done.1 = f32[2,384]{1,0:T(2,128)S(1)} collective-permute-done((f32[2,384]{1,0:T(2,128)S(1)}, f32[2,384]{1,0:T(2,128)S(1)}, u32[]{:S(2)}, u32[]{:S(2)}) %collective-permute-start.1) | collective-permute-done | bytes 3104 | tf_op jit(solution)/shard_map/ppermute | solution.py:274
  38.4 1.3 %collective-permute-start.6 = (f32[2,384]{1,0:T(2,128)S(1)}, f32[2,384]{1,0:T(2,128)S(1)}, u32[]{:S(2)}, u32[]{:S(2)}) collective-permute-start(f32[2,384]{1,0:T(2,128)S(1)} %add.24), channel_id=1, source_target_pairs={{448,0},{480,16},{449,1},{481,17},{450,2},{482,18},{451,3},{483,19... | collective-permute-start | bytes 9224 | tf_op jit(solution)/shard_map/ppermute | solution.py:274
  39.7 0.1 select_add_fusion
  39.7 0.6 %broadcast_in_dim.35 = f32[8,2,384]{2,1,0:T(2,128)} broadcast(f32[2,384]{1,0:T(2,128)S(1)} %select_add_fusion), dimensions={1,2} | broadcast | bytes 27648 | tf_op jit(solution)/shard_map/broadcast_in_dim | solution.py:289
  40.4 3.5 %all-to-all-start.1 = ((f32[8,2,384]{2,1,0:T(2,128)}), f32[8,2,384]{2,1,0:T(2,128)S(1)}, u32[]{:S(2)}, u32[]{:S(2)}) async-start(f32[8,2,384]{2,1,0:T(2,128)} %broadcast_in_dim.35), calls=%async_computation.1 | async-start | bytes 49152 | tf_op jit(solution)/shard_map/all_to_all | solution.py:291
  43.8 0.8 %shard_map.79 = (f32[286,128]{1,0:T(8,128)}, f32[26,286]{1,0:T(8,128)S(1)}) custom-call(f32[128,384]{1,0:T(8,128)S(1)} %get-tuple-element.19.held_ref, f32[80,384]{1,0:T(8,128)S(1)} %get-tuple-element.20.level_ref, s32[4,128]{1,0:T(4,128)S(1)} %get-tuple-element.21.span_ref), custom_call_target="tpu_custom_call" | custom-call | tf_op jit(solution)/shard_map/pallas_call | solution.py:306
  44.7 0.3 collective-permute-done.6
  45.0 1.2 %collective-permute-done.2 = f32[2,384]{1,0:T(2,128)S(1)} collective-permute-done((f32[2,384]{1,0:T(2,128)S(1)}, f32[2,384]{1,0:T(2,128)S(1)}, u32[]{:S(2)}, u32[]{:S(2)}) %collective-permute-start.2) | collective-permute-done | bytes 3104 | tf_op jit(solution)/shard_map/ppermute | solution.py:274
  46.2 0.4 collective-permute-done.5
  46.6 2.3 %collective-permute-start.7 = (f32[2,384]{1,0:T(2,128)S(1)}, f32[2,384]{1,0:T(2,128)S(1)}, u32[]{:S(2)}, u32[]{:S(2)}) collective-permute-start(f32[2,384]{1,0:T(2,128)S(1)} %add_add_fusion), channel_id=1, source_target_pairs={{16,0},{17,1},{18,2},{19,3},{20,4},{21,5},{22,6},{23,7},{24,8},{25... | collective-permute-start | bytes 9224 | tf_op jit(solution)/shard_map/ppermute | solution.py:274
  49.0 0.8 %collective-permute-done.7 = f32[2,384]{1,0:T(2,128)S(1)} collective-permute-done((f32[2,384]{1,0:T(2,128)S(1)}, f32[2,384]{1,0:T(2,128)S(1)}, u32[]{:S(2)}, u32[]{:S(2)}) %collective-permute-start.7) | collective-permute-done | bytes 3104 | tf_op jit(solution)/shard_map/ppermute | solution.py:274
  49.8 0.7 %select_multiply_fusion = f32[26,286]{1,0:T(8,128)} fusion(f32[26,286]{1,0:T(8,128)S(1)} %get-tuple-element.25, f32[286]{0:T(512)S(1)} %get-tuple-element.29, f32[286]{0:T(512)S(1)} %get-tuple-element.28, pred[26]{0:T(512)(128)(4,1)S(1)} %get-tuple-element.30, pred[26]{0:T(512)(128)(4,1)S(1)} %get-tuple-element.31), kind=kLoop, calls=%fused_computation | loop fusion | flops 22308 | bytes 61828 | tf_op jit(solution)/shard_map/mul | solution.py:360
  (13 shorter events, 0.1 us)
Async XLA Ops:
  4.4 17.4 %copy-start = (bf16[256,384]{1,0:T(8,128)(2,1)S(1)}, bf16[256,384]{1,0:T(8,128)(2,1)}, u32[]{:S(2)}) copy-start(bf16[256,384]{1,0:T(8,128)(2,1)} %constant.23.clone.shift_ref) | copy-start | bytes 589828
  4.4 17.4 %all-to-all-start = ((f32[16,72,128]{2,1,0:T(8,128)}), f32[16,72,128]{2,1,0:T(8,128)S(1)}, u32[]{:S(2)}, u32[]{:S(2)}) async-start(f32[16,72,128]{2,1,0:T(8,128)} %shard_map.77), calls=%async_computation | async-start | bytes 1179648 | tf_op jit(solution)/shard_map/all_to_all | solution.py:344
  12.1 9.7 %copy-start.1 = (f32[8,384]{1,0:T(8,128)S(1)}, f32[8,384]{1,0:T(8,128)}, u32[]{:S(2)}) copy-start(f32[8,384]{1,0:T(8,128)} %constant.24.clone.signs_ref) | copy-start | bytes 36868
  24.1 6.9 %collective-permute-start = (f32[2,384]{1,0:T(2,128)S(1)}, f32[2,384]{1,0:T(2,128)S(1)}, u32[]{:S(2)}, u32[]{:S(2)}) collective-permute-start(f32[2,384]{1,0:T(2,128)S(1)} %get-tuple-element.15), channel_id=1, source_target_pairs={{16,0},{48,32},{80,64},{112,96},{144,128},{176,160},{208,192},{240... | collective-permute-start | bytes 9224 | tf_op jit(solution)/shard_map/ppermute | solution.py:274
  29.6 8.7 %collective-permute-start.1 = (f32[2,384]{1,0:T(2,128)S(1)}, f32[2,384]{1,0:T(2,128)S(1)}, u32[]{:S(2)}, u32[]{:S(2)}) collective-permute-start(f32[2,384]{1,0:T(2,128)S(1)} %get-tuple-element.15), channel_id=1, source_target_pairs={{128,0},{144,16},{160,32},{176,48},{129,1},{145,17},{161,33},{177,... | collective-permute-start | bytes 9224 | tf_op jit(solution)/shard_map/ppermute | solution.py:274
  31.0 15.2 %collective-permute-start.2 = (f32[2,384]{1,0:T(2,128)S(1)}, f32[2,384]{1,0:T(2,128)S(1)}, u32[]{:S(2)}, u32[]{:S(2)}) collective-permute-start(f32[2,384]{1,0:T(2,128)S(1)} %add.24), channel_id=1, source_target_pairs={{256,0},{288,16},{257,1},{289,17},{258,2},{290,18},{259,3},{291,19... | collective-permute-start | bytes 9224 | tf_op jit(solution)/shard_map/ppermute | solution.py:274
  32.3 13.9 %collective-permute-start.3 = (f32[2,384]{1,0:T(2,128)S(1)}, f32[2,384]{1,0:T(2,128)S(1)}, u32[]{:S(2)}, u32[]{:S(2)}) collective-permute-start(f32[2,384]{1,0:T(2,128)S(1)} %add.24), channel_id=1, source_target_pairs={{320,0},{352,16},{321,1},{353,17},{322,2},{354,18},{323,3},{355,19... | collective-permute-start | bytes 9224 | tf_op jit(solution)/shard_map/ppermute | solution.py:274
  33.6 12.6 %collective-permute-start.4 = (f32[2,384]{1,0:T(2,128)S(1)}, f32[2,384]{1,0:T(2,128)S(1)}, u32[]{:S(2)}, u32[]{:S(2)}) collective-permute-start(f32[2,384]{1,0:T(2,128)S(1)} %add.24), channel_id=1, source_target_pairs={{384,0},{416,16},{385,1},{417,17},{386,2},{418,18},{387,3},{419,19... | collective-permute-start | bytes 9224 | tf_op jit(solution)/shard_map/ppermute | solution.py:274
  34.9 11.7 %collective-permute-start.5 = (f32[2,384]{1,0:T(2,128)S(1)}, f32[2,384]{1,0:T(2,128)S(1)}, u32[]{:S(2)}, u32[]{:S(2)}) collective-permute-start(f32[2,384]{1,0:T(2,128)S(1)} %add.24), channel_id=1, source_target_pairs={{192,0},{224,16},{193,1},{225,17},{194,2},{226,18},{195,3},{227,19... | collective-permute-start | bytes 9224 | tf_op jit(solution)/shard_map/ppermute | solution.py:274
  38.4 6.6 %collective-permute-start.6 = (f32[2,384]{1,0:T(2,128)S(1)}, f32[2,384]{1,0:T(2,128)S(1)}, u32[]{:S(2)}, u32[]{:S(2)}) collective-permute-start(f32[2,384]{1,0:T(2,128)S(1)} %add.24), channel_id=1, source_target_pairs={{448,0},{480,16},{449,1},{481,17},{450,2},{482,18},{451,3},{483,19... | collective-permute-start | bytes 9224 | tf_op jit(solution)/shard_map/ppermute | solution.py:274
  40.4 8.6 %all-to-all-start.1 = ((f32[8,2,384]{2,1,0:T(2,128)}), f32[8,2,384]{2,1,0:T(2,128)S(1)}, u32[]{:S(2)}, u32[]{:S(2)}) async-start(f32[8,2,384]{2,1,0:T(2,128)} %broadcast_in_dim.35), calls=%async_computation.1 | async-start | bytes 49152 | tf_op jit(solution)/shard_map/all_to_all | solution.py:291
  46.6 3.1 %collective-permute-start.7 = (f32[2,384]{1,0:T(2,128)S(1)}, f32[2,384]{1,0:T(2,128)S(1)}, u32[]{:S(2)}, u32[]{:S(2)}) collective-permute-start(f32[2,384]{1,0:T(2,128)S(1)} %add_add_fusion), channel_id=1, source_target_pairs={{16,0},{17,1},{18,2},{19,3},{20,4},{21,5},{22,6},{23,7},{24,8},{25... | collective-permute-start | bytes 9224 | tf_op jit(solution)/shard_map/ppermute | solution.py:274

commit v4 on v3

--- a/solution.py
+++ b/solution.py
@@ -124,24 +124,12 @@
         copy.wait()
 
 
-def tree_kernel(
-    where_ref, got_ref, shift_ref, signs_ref, send_ref, held_ref, level_ref, span_ref
-):
-    me = where_ref[0]
-    group = where_ref[1]
+def group_values(got_ref):
     lane = lax.broadcasted_iota(jnp.int32, (128, 128), 1)
     tails = got_ref[:, 64:72, :].reshape(128, 128)
-    turned = tails.T
-    dest_row = jnp.concatenate([turned[32 * g + 30 : 32 * g + 31] for g in range(4)], axis=1)
-    spot = lax.broadcasted_iota(jnp.int32, (1, GROUP), 1)
-    block_row = ((spot // 8) % 16) * 32 + (spot // 128) * 8 + spot % 8
-    key_row = dest_row * 512.0 + block_row.astype(F32)
-    spot = lax.broadcasted_iota(jnp.int32, (128, 1), 0)
-    high_parts, low_parts, pair_parts, key_parts = [], [], [], []
+    high_parts, low_parts, pair_parts = [], [], []
     for g in range(4):
         tail = tails if g == 0 else pltpu.roll(tails, 128 - 32 * g, 1)
-        block = (spot // 8) * 32 + g * 8 + spot % 8
-        key_parts.append(tail[:, 30:31] * 512.0 + block.astype(F32))
         first = got_ref[:, 8 * g : 8 * g + 8, :].reshape(128, 128)
         second = got_ref[:, 32 + 8 * g : 40 + 8 * g, :].reshape(128, 128)
         tail = jnp.where(lane < 30, tail, 0.0)
@@ -151,14 +139,27 @@
         high_parts.append(jnp.concatenate([first_high, second_high], axis=1))
         low_parts.append(jnp.concatenate([first_low, second_low], axis=1))
         pair_parts.append(pair.astype(BF16))
-    held = jnp.concatenate(
-        [
-            jnp.concatenate(high_parts, axis=0),
-            jnp.concatenate(low_parts, axis=0),
-            jnp.concatenate(pair_parts, axis=0),
-        ],
-        axis=1,
-    )
+    parts = [jnp.concatenate(p, axis=0) for p in (high_parts, low_parts, pair_parts)]
+    return jnp.concatenate(parts, axis=1)
+
+
+def tree_kernel(
+    where_ref, got_ref, shift_ref, signs_ref, send_ref, rank_ref, level_ref, span_ref
+):
+    me = where_ref[0]
+    group = where_ref[1]
+    tails = got_ref[:, 64:72, :].reshape(128, 128)
+    turned = tails.T
+    dest_row = jnp.concatenate([turned[32 * g + 30 : 32 * g + 31] for g in range(4)], axis=1)
+    spot = lax.broadcasted_iota(jnp.int32, (1, GROUP), 1)
+    block_row = ((spot // 8) % 16) * 32 + (spot // 128) * 8 + spot % 8
+    key_row = dest_row * 512.0 + block_row.astype(F32)
+    spot = lax.broadcasted_iota(jnp.int32, (128, 1), 0)
+    key_parts = []
+    for g in range(4):
+        block = (spot // 8) * 32 + g * 8 + spot % 8
+        key_parts.append(tails[:, 32 * g + 30 : 32 * g + 31] * 512.0 + block.astype(F32))
+    held = group_values(got_ref)
     smaller = jnp.zeros((8, GROUP), F32)
     for g in range(4):
         less = jnp.where(key_parts[g] < key_row, 1.0, 0.0)
@@ -169,14 +170,9 @@
     tally = jnp.sum(jnp.where(dest_row == mine, 1.0, 0.0), axis=1, keepdims=True).astype(jnp.int32)
     row = lax.broadcasted_iota(jnp.int32, (GROUP, 1), 0)
     turned_row = (row % 8) * 64 + ((row // 8) % 8) * 8 + row // 64
-    slot = lax.broadcasted_iota(jnp.int32, (128, 1), 0)
-    wanted = jnp.concatenate([turned_row, jnp.where(slot < tally, start + slot, -1)], axis=0)
-    chosen = jnp.where(wanted == rank, 1.0, 0.0).astype(BF16)
-    placed = jnp.dot(chosen, held, preferred_element_type=F32)
-    own = placed[GROUP:]
-    own_tail = own[:, 512:640]
-    held_ref[:, 0:256] = own[:, 0:256] + own[:, 256:512]
-    held_ref[:, 256:384] = own_tail + pltpu.roll(own_tail, 96, 1)
+    chosen = jnp.where(turned_row == rank, 1.0, 0.0).astype(BF16)
+    sons = jnp.dot(chosen, held, preferred_element_type=F32)
+    rank_ref[...] = rank
     shift = shift_ref[...]
     tiny = 2.0**-P_SIZE
 
@@ -193,7 +189,6 @@
     sign_rows = jnp.concatenate(
         [jnp.broadcast_to(signed(o)[:, 0:256], (64, 256)) for o in range(8)], axis=0
     )
-    sons = placed[:GROUP]
     high = (sons[:, 0:256] * sign_rows).astype(BF16)
     low = (sons[:, 256:512] * sign_rows).astype(BF16)
     parts = moved(high, low)
@@ -242,13 +237,16 @@
     span_ref[3:4] = jnp.zeros((1, 128), jnp.int32) + jnp.where(group == 0, 24, -1)
 
 
-def outputs_kernel(held_ref, level_ref, span_ref, leaf_ref, box_ref):
-    held = held_ref[...]
-    leaf_ref[0:128] = held[:, 0:128].T
-    leaf_ref[128:256] = held[:, 128:256].T
-    leaf_ref[256:COEFS] = held[:, 256:384].T[0 : COEFS - 256]
+def outputs_kernel(got_ref, rank_ref, level_ref, span_ref, leaf_ref, box_ref):
     start = span_ref[0:1, 0:1]
     end = span_ref[1:2, 0:1]
+    slot = start + lax.broadcasted_iota(jnp.int32, (128, 1), 0)
+    chosen = jnp.where(jnp.where(slot < end, slot, -1) == rank_ref[...], 1.0, 0.0).astype(BF16)
+    own = jnp.dot(chosen, group_values(got_ref), preferred_element_type=F32)
+    own_tail = own[:, 512:640]
+    leaf_ref[0:128] = (own[:, 0:128] + own[:, 256:384]).T
+    leaf_ref[128:256] = (own[:, 128:256] + own[:, 384:512]).T
+    leaf_ref[256:COEFS] = (own_tail + pltpu.roll(own_tail, 96, 1)).T[0 : COEFS - 256]
     out_slot = lax.broadcasted_iota(jnp.int32, (32, 1), 0)
     box_1 = start // 8 + out_slot
     box_2 = start // 64 + out_slot - 17
@@ -274,26 +272,25 @@
     return lax.ppermute(value, "wide", list(pairs))
 
 
-def across(share, kept):
-    four = permute(share, *((8 + i, i) for i in range(4)))
+def across(share, got, kept):
+    four = permute(share, *((8 + i, i) for i in range(6)))
     pair = share + permute(share, *((2 * i + 1, 2 * i) for i in range(16)))
-    eight = permute(pair, (16, 0), (18, 1))
-    ten = permute(pair, (20, 0), (22, 1))
+    eight = permute(pair, (16, 0))
+    nine = permute(pair, (18, 1), (20, 0))
+    seven = permute(pair, (14, 0), (22, 1))
     twelve = permute(pair, (24, 0), (26, 1))
-    six = permute(pair, (12, 0), (14, 1))
     after, four, kept = lax.optimization_barrier((pair, four, kept))
     fourteen = permute(after, (28, 0), (30, 1))
-    row = lax.broadcasted_iota(jnp.int32, (2, 384), 0)
-    mixed = share + jnp.where(row == 0, 0.0, four)
     quads = [[8 * q + j for j in range(8)] for q in range(4)]
-    spread = jnp.broadcast_to(mixed[None], (8, 2, 384))
+    row = lax.broadcasted_iota(jnp.int32, (8, 2, 384), 1)
+    spread = share[None] + jnp.where(row == 0, 0.0, four[None])
     quad = jnp.sum(
         lax.all_to_all(spread, "wide", 0, 0, axis_index_groups=quads, tiled=True), axis=0
     )
-    leaf, box = outputs(*kept)
-    late = eight + ten + twelve + six + fourteen
+    leaf, box = outputs(got, *kept)
+    late = twelve + seven + nine + fourteen
     late, box = lax.optimization_barrier((late, box))
-    return quad, quad + late + permute(late, (1, 0)), leaf, box
+    return quad, quad + late + eight + permute(late, (1, 0)), leaf, box
 
 
 VMEM = pl.BlockSpec(memory_space=pltpu.VMEM)
@@ -302,17 +299,17 @@
 PARAMS = pltpu.CompilerParams(vmem_limit_bytes=40 * 1024 * 1024)
 
 
-def outputs(held, levels, span):
+def outputs(got, rank, levels, span):
     return pl.pallas_call(
         outputs_kernel,
         out_shape=(
             jax.ShapeDtypeStruct((COEFS, 128), F32),
             jax.ShapeDtypeStruct((26, COEFS), F32),
         ),
-        in_specs=[VMEM] * 3,
+        in_specs=[VMEM] * 4,
         out_specs=(VMEM,) * 2,
         compiler_params=PARAMS,
-    )(held, levels, span)
+    )(got, rank, levels, span)
 
 
 def shards(positions, moments, counts, dest):
@@ -346,7 +343,7 @@
         tree_kernel,
         out_shape=(
             jax.ShapeDtypeStruct((2, 384), F32),
-            jax.ShapeDtypeStruct((128, 384), F32),
+            jax.ShapeDtypeStruct((1, GROUP), jnp.int32),
             jax.ShapeDtypeStruct((80, 384), F32),
             jax.ShapeDtypeStruct((4, 128), jnp.int32),
         ),
@@ -354,7 +351,7 @@
         out_specs=(VMEM,) * 4,
         compiler_params=PARAMS,
     )(where, got, jnp.asarray(shift, BF16), jnp.asarray(signs, F32))
-    quad, top, leaf, box = across(share, kept)
+    quad, top, leaf, box = across(share, got, kept)
     row = lax.broadcasted_iota(jnp.int32, (26, COEFS), 0)
     last = jnp.where(row == 24, top[1:2, 0:COEFS], 1.0)
     box = box * jnp.where(row == 22, quad[0:1, 0:COEFS], last)

time: 51 us -> 50.5 us (level)
  other arithmetic: 0.92 us -> 1.54 us
  local copies, waits for them, and re-layouts: 0.63 us -> 0.01 us
    ppermute x8, waiting for transfers between devices: 4.89 us -> 3.39 us  [permute(): return lax.ppermute(value, 'wide', list(pairs))]
    all_to_all x1, waiting for transfers between devices: 0.01 us -> 1.3 us  [across(): lax.all_to_all(spread, 'wide', 0, 0, axis_index_groups=quads, tiled=True)]
    ppermute x8, starting transfers between devices: 15.6 us -> 14.5 us  [permute(): return lax.ppermute(value, 'wide', list(pairs))]
    all_to_all x1, starting transfers between devices: 3.5 us -> 4.17 us  [across(): lax.all_to_all(spread, 'wide', 0, 0, axis_index_groups=quads, tiled=True)]
    broadcast_in_dim x1 -> x0, local copies, waits for them, and re-layouts: 0.62 us -> none  [across(): spread = jnp.broadcast_to(mixed[None], (8, 2, 384))]
    add x2, other arithmetic: 0.08 us -> 0.69 us  [the longest x1 0.69 us: across(): spread = share[None] + jnp.where(row == 0, 0.0, four[None])]
  transfers between devices with their start and end apart: 10 -> 10, of which waited for: 6 -> 5; matrix products, arithmetic and copies ran while one was open for 2% -> 2% of each run, Pallas kernels for 2% -> 2%
where the time goes in v4:
time: 50.5 us; the launch traced here: 50 us
  starting transfers between devices  26.4 us (52%)
  waiting for transfers between devices  14.2 us (28%)
  Pallas kernels  7.06 us (14%)
  other arithmetic  1.54 us (3%)
  between operations  0.78 us (2%)
    ppermute x8, starting transfers between devices, permute(): return lax.ppermute(value, 'wide', list(pairs))  14.5 us
    all_to_all x1, waiting for transfers between devices, shards(): lax.all_to_all(sent, 'narrow', split_axis=0, concat_axis=0, tiled=True)  9.56 us
    all_to_all x1, starting transfers between devices, shards(): lax.all_to_all(sent, 'narrow', split_axis=0, concat_axis=0, tiled=True)  7.73 us
    all_to_all x1, starting transfers between devices, across(): lax.all_to_all(spread, 'wide', 0, 0, axis_index_groups=quads, tiled=True)  4.17 us
    pallas_call x1, Pallas kernels, shards(): pl.pallas_call(moments_kernel, out_shape=jax.ShapeDtypeStruct((16, 72, 12...  3.76 us
    ppermute x8, waiting for transfers between devices, permute(): return lax.ppermute(value, 'wide', list(pairs))  3.39 us
    pallas_call x1, Pallas kernels, shards(): pl.pallas_call(tree_kernel, out_shape=(jax.ShapeDtypeStruct((2, 384), F32...  2.05 us
    all_to_all x1, waiting for transfers between devices, across(): lax.all_to_all(spread, 'wide', 0, 0, axis_index_groups=quads, tiled=True)  1.3 us
  transfers between devices with their start and end apart: 10, of which 5 were waited for; matrix products, arithmetic and copies ran while one was open for 2% of the time, Pallas kernels for 2%

profile of v4, /device:TPU:1, one launch (start us, length us, event | category | flops | bytes accessed | tf_op | source)
XLA Modules:
  0.0 50.0 jit_solution(14215451423300751953)
XLA Ops:
  0.6 3.8 %shard_map.77 = f32[16,72,128]{2,1,0:T(8,128)} custom-call(f32[3,32,256]{2,1,0:T(8,128)} %bitcast.7, f32[3,32,256]{2,1,0:T(8,128)} %bitcast.8, s32[1,32]{1,0:T(1,128)} %bitcast.9, s32[1,32]{1,0:T(1,128)} %bitcast.10), custom_call_target="tpu_custom_call" | custom-call | tf_op jit(solution)/shard_map/pallas_call | solution.py:318
  4.4 0.0 copy-start
  4.4 7.7 %all-to-all-start = ((f32[16,72,128]{2,1,0:T(8,128)}), f32[16,72,128]{2,1,0:T(8,128)S(1)}, u32[]{:S(2)}, u32[]{:S(2)}) async-start(f32[16,72,128]{2,1,0:T(8,128)} %shard_map.77), calls=%async_computation | async-start | bytes 1179648 | tf_op jit(solution)/shard_map/all_to_all | solution.py:341
  12.1 0.0 copy-start.1
  12.2 0.1 pad_add_fusion.where_ref
  12.2 9.6 %all-to-all-done.got_ref = f32[16,72,128]{2,1,0:T(8,128)S(1)} async-done(((f32[16,72,128]{2,1,0:T(8,128)}), f32[16,72,128]{2,1,0:T(8,128)S(1)}, u32[]{:S(2)}, u32[]{:S(2)}) %all-to-all-start) | async-done | bytes 589856 | tf_op jit(solution)/shard_map/all_to_all | solution.py:341
  21.8 2.0 %shard_map.78 = (f32[2,384]{1,0:T(2,128)S(1)}, s32[1,512]{1,0:T(1,128)S(1)}, f32[80,384]{1,0:T(8,128)S(1)}, s32[4,128]{1,0:T(4,128)S(1)}) custom-call(s32[2]{0:T(128)S(1)} %pad_add_fusion.where_ref, f32[16,72,128]{2,1,0:T(8,128)S(1)} %all-to-all-done.got_ref, bf16[256,384]{1,0:T(8,128)(2,1)S(1)} %copy-done, f32[8,384]{1,0:T(8,128)S(1)} %copy-done.1), custom_call_target="tpu_custom_call" | custom-call | tf_op jit(solution)/shard_map/pallas_call | solution.py:342
  23.8 5.5 %collective-permute-start = (f32[2,384]{1,0:T(2,128)S(1)}, f32[2,384]{1,0:T(2,128)S(1)}, u32[]{:S(2)}, u32[]{:S(2)}) collective-permute-start(f32[2,384]{1,0:T(2,128)S(1)} %get-tuple-element.15), channel_id=1, source_target_pairs={{16,0},{48,32},{80,64},{112,96},{144,128},{176,160},{208,192},{240... | collective-permute-start | bytes 9224 | tf_op jit(solution)/shard_map/ppermute | solution.py:272
  29.4 1.3 %collective-permute-start.1 = (f32[2,384]{1,0:T(2,128)S(1)}, f32[2,384]{1,0:T(2,128)S(1)}, u32[]{:S(2)}, u32[]{:S(2)}) collective-permute-start(f32[2,384]{1,0:T(2,128)S(1)} %get-tuple-element.15), channel_id=1, source_target_pairs={{128,0},{144,16},{160,32},{176,48},{192,64},{208,80},{129,1},{145,... | collective-permute-start | bytes 9224 | tf_op jit(solution)/shard_map/ppermute | solution.py:272
  30.7 1.3 %collective-permute-start.4 = (f32[2,384]{1,0:T(2,128)S(1)}, f32[2,384]{1,0:T(2,128)S(1)}, u32[]{:S(2)}, u32[]{:S(2)}) collective-permute-start(f32[2,384]{1,0:T(2,128)S(1)} %add.29), channel_id=1, source_target_pairs={{288,16},{320,0},{289,17},{321,1},{290,18},{322,2},{291,19},{323,3... | collective-permute-start | bytes 9224 | tf_op jit(solution)/shard_map/ppermute | solution.py:272
  32.0 1.3 %collective-permute-start.2 = (f32[2,384]{1,0:T(2,128)S(1)}, f32[2,384]{1,0:T(2,128)S(1)}, u32[]{:S(2)}, u32[]{:S(2)}) collective-permute-start(f32[2,384]{1,0:T(2,128)S(1)} %add.29), channel_id=1, source_target_pairs={{384,0},{416,16},{385,1},{417,17},{386,2},{418,18},{387,3},{419,19... | collective-permute-start | bytes 9224 | tf_op jit(solution)/shard_map/ppermute | solution.py:272
  33.3 1.3 %collective-permute-start.3 = (f32[2,384]{1,0:T(2,128)S(1)}, f32[2,384]{1,0:T(2,128)S(1)}, u32[]{:S(2)}, u32[]{:S(2)}) collective-permute-start(f32[2,384]{1,0:T(2,128)S(1)} %add.29), channel_id=1, source_target_pairs={{224,0},{352,16},{225,1},{353,17},{226,2},{354,18},{227,3},{355,19... | collective-permute-start | bytes 9224 | tf_op jit(solution)/shard_map/ppermute | solution.py:272
  34.6 0.7 %collective-permute-start.6 = (f32[2,384]{1,0:T(2,128)S(1)}, f32[2,384]{1,0:T(2,128)S(1)}, u32[]{:S(2)}, u32[]{:S(2)}) collective-permute-start(f32[2,384]{1,0:T(2,128)S(1)} %add.29), channel_id=1, source_target_pairs={{256,0},{257,1},{258,2},{259,3},{260,4},{261,5},{262,6},{263,7},{2... | collective-permute-start | bytes 9224 | tf_op jit(solution)/shard_map/ppermute | solution.py:272
  35.3 2.8 %collective-permute-done.1 = f32[2,384]{1,0:T(2,128)S(1)} collective-permute-done((f32[2,384]{1,0:T(2,128)S(1)}, f32[2,384]{1,0:T(2,128)S(1)}, u32[]{:S(2)}, u32[]{:S(2)}) %collective-permute-start.1) | collective-permute-done | bytes 3104 | tf_op jit(solution)/shard_map/ppermute | solution.py:272
  38.1 1.3 %collective-permute-start.5 = (f32[2,384]{1,0:T(2,128)S(1)}, f32[2,384]{1,0:T(2,128)S(1)}, u32[]{:S(2)}, u32[]{:S(2)}) collective-permute-start(f32[2,384]{1,0:T(2,128)S(1)} %add.29), channel_id=1, source_target_pairs={{448,0},{480,16},{449,1},{481,17},{450,2},{482,18},{451,3},{483,19... | collective-permute-start | bytes 9224 | tf_op jit(solution)/shard_map/ppermute | solution.py:272
  39.4 0.7 %select_add_fusion = f32[8,2,384]{2,1,0:T(2,128)} fusion(pred[2]{0:T(512)(128)(4,1)S(1)} %iota_compare_fusion.1, f32[2,384]{1,0:T(2,128)S(1)} %collective-permute-done.1, f32[2,384]{1,0:T(2,128)S(1)} %get-tuple-element.15), kind=kLoop, calls=%fused_computation.1 | loop fusion | flops 12288 | bytes 30722 | tf_op jit(solution)/shard_map/add | solution.py:286
  40.1 4.2 %all-to-all-start.1 = ((f32[8,2,384]{2,1,0:T(2,128)}), f32[8,2,384]{2,1,0:T(2,128)S(1)}, u32[]{:S(2)}, u32[]{:S(2)}) async-start(f32[8,2,384]{2,1,0:T(2,128)} %select_add_fusion), calls=%async_computation.1 | async-start | bytes 49152 | tf_op jit(solution)/shard_map/all_to_all | solution.py:288
  44.3 1.2 %shard_map.79 = (f32[286,128]{1,0:T(8,128)}, f32[26,286]{1,0:T(8,128)S(1)}) custom-call(f32[16,72,128]{2,1,0:T(8,128)S(1)} %all-to-all-done.got_ref, s32[1,512]{1,0:T(1,128)S(1)} %get-tuple-element.19.rank_ref, f32[80,384]{1,0:T(8,128)S(1)} %get-tuple-element.20.level_ref, s32[4,128]{1,0:T(4,128)S(1)} %get-tuple-element.21.span_ref), custom_call_target="tpu_custom_call" | custom-call | tf_op jit(solution)/shard_map/pallas_call | solution.py:303
  45.5 0.0 collective-permute-done.5
  45.5 0.1 collective-permute-done.4
  45.6 0.4 collective-permute-done.3
  46.1 1.8 %collective-permute-start.7 = (f32[2,384]{1,0:T(2,128)S(1)}, f32[2,384]{1,0:T(2,128)S(1)}, u32[]{:S(2)}, u32[]{:S(2)}) collective-permute-start(f32[2,384]{1,0:T(2,128)S(1)} %add_add_fusion), channel_id=1, source_target_pairs={{16,0},{17,1},{18,2},{19,3},{20,4},{21,5},{22,6},{23,7},{24,8},{25... | collective-permute-start | bytes 9224 | tf_op jit(solution)/shard_map/ppermute | solution.py:272
  47.9 1.3 %all-to-all-done.1 = f32[8,2,384]{2,1,0:T(2,128)S(1)} async-done(((f32[8,2,384]{2,1,0:T(2,128)}), f32[8,2,384]{2,1,0:T(2,128)S(1)}, u32[]{:S(2)}, u32[]{:S(2)}) %all-to-all-start.1) | async-done | bytes 24608 | tf_op jit(solution)/shard_map/all_to_all | solution.py:288
  49.3 0.7 %select_multiply_fusion = f32[26,286]{1,0:T(8,128)} fusion(f32[26,286]{1,0:T(8,128)S(1)} %get-tuple-element.25, f32[286]{0:T(512)S(1)} %get-tuple-element.29, f32[286]{0:T(512)S(1)} %get-tuple-element.28, pred[26]{0:T(512)(128)(4,1)S(1)} %get-tuple-element.30, pred[26]{0:T(512)(128)(4,1)S(1)} %get-tuple-element.31), kind=kLoop, calls=%fused_computation | loop fusion | flops 22308 | bytes 61828 | tf_op jit(solution)/shard_map/mul | solution.py:357
  (12 shorter events, 0.1 us)
Async XLA Ops:
  4.4 17.4 %copy-start = (bf16[256,384]{1,0:T(8,128)(2,1)S(1)}, bf16[256,384]{1,0:T(8,128)(2,1)}, u32[]{:S(2)}) copy-start(bf16[256,384]{1,0:T(8,128)(2,1)} %constant.23.clone.shift_ref) | copy-start | bytes 589828
  4.4 17.4 %all-to-all-start = ((f32[16,72,128]{2,1,0:T(8,128)}), f32[16,72,128]{2,1,0:T(8,128)S(1)}, u32[]{:S(2)}, u32[]{:S(2)}) async-start(f32[16,72,128]{2,1,0:T(8,128)} %shard_map.77), calls=%async_computation | async-start | bytes 1179648 | tf_op jit(solution)/shard_map/all_to_all | solution.py:341
  12.1 9.7 %copy-start.1 = (f32[8,384]{1,0:T(8,128)S(1)}, f32[8,384]{1,0:T(8,128)}, u32[]{:S(2)}) copy-start(f32[8,384]{1,0:T(8,128)} %constant.24.clone.signs_ref) | copy-start | bytes 36868
  23.8 6.9 %collective-permute-start = (f32[2,384]{1,0:T(2,128)S(1)}, f32[2,384]{1,0:T(2,128)S(1)}, u32[]{:S(2)}, u32[]{:S(2)}) collective-permute-start(f32[2,384]{1,0:T(2,128)S(1)} %get-tuple-element.15), channel_id=1, source_target_pairs={{16,0},{48,32},{80,64},{112,96},{144,128},{176,160},{208,192},{240... | collective-permute-start | bytes 9224 | tf_op jit(solution)/shard_map/ppermute | solution.py:272
  29.4 8.7 %collective-permute-start.1 = (f32[2,384]{1,0:T(2,128)S(1)}, f32[2,384]{1,0:T(2,128)S(1)}, u32[]{:S(2)}, u32[]{:S(2)}) collective-permute-start(f32[2,384]{1,0:T(2,128)S(1)} %get-tuple-element.15), channel_id=1, source_target_pairs={{128,0},{144,16},{160,32},{176,48},{192,64},{208,80},{129,1},{145,... | collective-permute-start | bytes 9224 | tf_op jit(solution)/shard_map/ppermute | solution.py:272
  30.7 14.9 %collective-permute-start.4 = (f32[2,384]{1,0:T(2,128)S(1)}, f32[2,384]{1,0:T(2,128)S(1)}, u32[]{:S(2)}, u32[]{:S(2)}) collective-permute-start(f32[2,384]{1,0:T(2,128)S(1)} %add.29), channel_id=1, source_target_pairs={{288,16},{320,0},{289,17},{321,1},{290,18},{322,2},{291,19},{323,3... | collective-permute-start | bytes 9224 | tf_op jit(solution)/shard_map/ppermute | solution.py:272
  32.0 13.6 %collective-permute-start.2 = (f32[2,384]{1,0:T(2,128)S(1)}, f32[2,384]{1,0:T(2,128)S(1)}, u32[]{:S(2)}, u32[]{:S(2)}) collective-permute-start(f32[2,384]{1,0:T(2,128)S(1)} %add.29), channel_id=1, source_target_pairs={{384,0},{416,16},{385,1},{417,17},{386,2},{418,18},{387,3},{419,19... | collective-permute-start | bytes 9224 | tf_op jit(solution)/shard_map/ppermute | solution.py:272
  33.3 12.8 %collective-permute-start.3 = (f32[2,384]{1,0:T(2,128)S(1)}, f32[2,384]{1,0:T(2,128)S(1)}, u32[]{:S(2)}, u32[]{:S(2)}) collective-permute-start(f32[2,384]{1,0:T(2,128)S(1)} %add.29), channel_id=1, source_target_pairs={{224,0},{352,16},{225,1},{353,17},{226,2},{354,18},{227,3},{355,19... | collective-permute-start | bytes 9224 | tf_op jit(solution)/shard_map/ppermute | solution.py:272
  34.6 14.6 %collective-permute-start.6 = (f32[2,384]{1,0:T(2,128)S(1)}, f32[2,384]{1,0:T(2,128)S(1)}, u32[]{:S(2)}, u32[]{:S(2)}) collective-permute-start(f32[2,384]{1,0:T(2,128)S(1)} %add.29), channel_id=1, source_target_pairs={{256,0},{257,1},{258,2},{259,3},{260,4},{261,5},{262,6},{263,7},{2... | collective-permute-start | bytes 9224 | tf_op jit(solution)/shard_map/ppermute | solution.py:272
  38.1 7.4 %collective-permute-start.5 = (f32[2,384]{1,0:T(2,128)S(1)}, f32[2,384]{1,0:T(2,128)S(1)}, u32[]{:S(2)}, u32[]{:S(2)}) collective-permute-start(f32[2,384]{1,0:T(2,128)S(1)} %add.29), channel_id=1, source_target_pairs={{448,0},{480,16},{449,1},{481,17},{450,2},{482,18},{451,3},{483,19... | collective-permute-start | bytes 9224 | tf_op jit(solution)/shard_map/ppermute | solution.py:272
  40.1 9.1 %all-to-all-start.1 = ((f32[8,2,384]{2,1,0:T(2,128)}), f32[8,2,384]{2,1,0:T(2,128)S(1)}, u32[]{:S(2)}, u32[]{:S(2)}) async-start(f32[8,2,384]{2,1,0:T(2,128)} %select_add_fusion), calls=%async_computation.1 | async-start | bytes 49152 | tf_op jit(solution)/shard_map/all_to_all | solution.py:288
  46.1 3.2 %collective-permute-start.7 = (f32[2,384]{1,0:T(2,128)S(1)}, f32[2,384]{1,0:T(2,128)S(1)}, u32[]{:S(2)}, u32[]{:S(2)}) collective-permute-start(f32[2,384]{1,0:T(2,128)S(1)} %add_add_fusion), channel_id=1, source_target_pairs={{16,0},{17,1},{18,2},{19,3},{20,4},{21,5},{22,6},{23,7},{24,8},{25... | collective-permute-start | bytes 9224 | tf_op jit(solution)/shard_map/ppermute | solution.py:272

commit v5 on v4

--- a/solution.py
+++ b/solution.py
@@ -288,8 +288,7 @@
         lax.all_to_all(spread, "wide", 0, 0, axis_index_groups=quads, tiled=True), axis=0
     )
     leaf, box = outputs(got, *kept)
-    late = twelve + seven + nine + fourteen
-    late, box = lax.optimization_barrier((late, box))
+    late = seven + twelve + nine + fourteen
     return quad, quad + late + eight + permute(late, (1, 0)), leaf, box
 
 

time: 50.5 us -> 50.5 us (level)
    all_to_all x1, waiting for transfers between devices: 1.3 us -> 0.04 us  [across(): lax.all_to_all(spread, 'wide', 0, 0, axis_index_groups=quads, tiled=True)]
    ppermute x8, waiting for transfers between devices: 3.39 us -> 4.2 us  [permute(): return lax.ppermute(value, 'wide', list(pairs))]
  transfers between devices with their start and end apart: 10 -> 10, of which waited for: 5 -> 4; matrix products, arithmetic and copies ran while one was open for 2% -> 2% of each run, Pallas kernels for 2% -> 3%
where the time goes in v5:
time: 50.5 us; the launch traced here: 50 us
  starting transfers between devices  26.8 us (53%)
  waiting for transfers between devices  13.8 us (27%)
  Pallas kernels  7.06 us (14%)
  other arithmetic  1.54 us (3%)
  between operations  0.79 us (2%)
    ppermute x8, starting transfers between devices, permute(): return lax.ppermute(value, 'wide', list(pairs))  14.9 us
    all_to_all x1, waiting for transfers between devices, shards(): lax.all_to_all(sent, 'narrow', split_axis=0, concat_axis=0, tiled=True)  9.56 us
    all_to_all x1, starting transfers between devices, shards(): lax.all_to_all(sent, 'narrow', split_axis=0, concat_axis=0, tiled=True)  7.73 us
    ppermute x8, waiting for transfers between devices, permute(): return lax.ppermute(value, 'wide', list(pairs))  4.2 us
    all_to_all x1, starting transfers between devices, across(): lax.all_to_all(spread, 'wide', 0, 0, axis_index_groups=quads, tiled=True)  4.17 us
    pallas_call x1, Pallas kernels, shards(): pl.pallas_call(moments_kernel, out_shape=jax.ShapeDtypeStruct((16, 72, 12...  3.76 us
    pallas_call x1, Pallas kernels, shards(): pl.pallas_call(tree_kernel, out_shape=(jax.ShapeDtypeStruct((2, 384), F32...  2.05 us
    pallas_call x1, Pallas kernels, outputs(): pl.pallas_call(outputs_kernel, out_shape=(jax.ShapeDtypeStruct((COEFS, 12...  1.25 us
  transfers between devices with their start and end apart: 10, of which 4 were waited for; matrix products, arithmetic and copies ran while one was open for 2% of the time, Pallas kernels for 3%

profile of v5, /device:TPU:1, one launch (start us, length us, event | category | flops | bytes accessed | tf_op | source)
XLA Modules:
  0.0 50.0 jit_solution(6255990560052589795)
XLA Ops:
  0.6 3.8 %shard_map.77 = f32[16,72,128]{2,1,0:T(8,128)} custom-call(f32[3,32,256]{2,1,0:T(8,128)} %bitcast.7, f32[3,32,256]{2,1,0:T(8,128)} %bitcast.8, s32[1,32]{1,0:T(1,128)} %bitcast.9, s32[1,32]{1,0:T(1,128)} %bitcast.10), custom_call_target="tpu_custom_call" | custom-call | tf_op jit(solution)/shard_map/pallas_call | solution.py:317
  4.4 0.0 copy-start
  4.4 7.7 %all-to-all-start = ((f32[16,72,128]{2,1,0:T(8,128)}), f32[16,72,128]{2,1,0:T(8,128)S(1)}, u32[]{:S(2)}, u32[]{:S(2)}) async-start(f32[16,72,128]{2,1,0:T(8,128)} %shard_map.77), calls=%async_computation | async-start | bytes 1179648 | tf_op jit(solution)/shard_map/all_to_all | solution.py:340
  12.1 0.0 copy-start.1
  12.2 0.1 pad_add_fusion.where_ref
  12.2 9.6 %all-to-all-done.got_ref = f32[16,72,128]{2,1,0:T(8,128)S(1)} async-done(((f32[16,72,128]{2,1,0:T(8,128)}), f32[16,72,128]{2,1,0:T(8,128)S(1)}, u32[]{:S(2)}, u32[]{:S(2)}) %all-to-all-start) | async-done | bytes 589856 | tf_op jit(solution)/shard_map/all_to_all | solution.py:340
  21.8 2.0 %shard_map.78 = (f32[2,384]{1,0:T(2,128)S(1)}, s32[1,512]{1,0:T(1,128)S(1)}, f32[80,384]{1,0:T(8,128)S(1)}, s32[4,128]{1,0:T(4,128)S(1)}) custom-call(s32[2]{0:T(128)S(1)} %pad_add_fusion.where_ref, f32[16,72,128]{2,1,0:T(8,128)S(1)} %all-to-all-done.got_ref, bf16[256,384]{1,0:T(8,128)(2,1)S(1)} %copy-done, f32[8,384]{1,0:T(8,128)S(1)} %copy-done.1), custom_call_target="tpu_custom_call" | custom-call | tf_op jit(solution)/shard_map/pallas_call | solution.py:341
  23.8 5.5 %collective-permute-start = (f32[2,384]{1,0:T(2,128)S(1)}, f32[2,384]{1,0:T(2,128)S(1)}, u32[]{:S(2)}, u32[]{:S(2)}) collective-permute-start(f32[2,384]{1,0:T(2,128)S(1)} %get-tuple-element.13), channel_id=1, source_target_pairs={{16,0},{48,32},{80,64},{112,96},{144,128},{176,160},{208,192},{240... | collective-permute-start | bytes 9224 | tf_op jit(solution)/shard_map/ppermute | solution.py:272
  29.4 1.3 %collective-permute-start.1 = (f32[2,384]{1,0:T(2,128)S(1)}, f32[2,384]{1,0:T(2,128)S(1)}, u32[]{:S(2)}, u32[]{:S(2)}) collective-permute-start(f32[2,384]{1,0:T(2,128)S(1)} %get-tuple-element.13), channel_id=1, source_target_pairs={{128,0},{144,16},{160,32},{176,48},{192,64},{208,80},{129,1},{145,... | collective-permute-start | bytes 9224 | tf_op jit(solution)/shard_map/ppermute | solution.py:272
  30.7 1.3 %collective-permute-start.4 = (f32[2,384]{1,0:T(2,128)S(1)}, f32[2,384]{1,0:T(2,128)S(1)}, u32[]{:S(2)}, u32[]{:S(2)}) collective-permute-start(f32[2,384]{1,0:T(2,128)S(1)} %add.29), channel_id=1, source_target_pairs={{288,16},{320,0},{289,17},{321,1},{290,18},{322,2},{291,19},{323,3... | collective-permute-start | bytes 9224 | tf_op jit(solution)/shard_map/ppermute | solution.py:272
  32.0 1.3 %collective-permute-start.2 = (f32[2,384]{1,0:T(2,128)S(1)}, f32[2,384]{1,0:T(2,128)S(1)}, u32[]{:S(2)}, u32[]{:S(2)}) collective-permute-start(f32[2,384]{1,0:T(2,128)S(1)} %add.29), channel_id=1, source_target_pairs={{224,0},{352,16},{225,1},{353,17},{226,2},{354,18},{227,3},{355,19... | collective-permute-start | bytes 9224 | tf_op jit(solution)/shard_map/ppermute | solution.py:272
  33.3 1.3 %collective-permute-start.3 = (f32[2,384]{1,0:T(2,128)S(1)}, f32[2,384]{1,0:T(2,128)S(1)}, u32[]{:S(2)}, u32[]{:S(2)}) collective-permute-start(f32[2,384]{1,0:T(2,128)S(1)} %add.29), channel_id=1, source_target_pairs={{384,0},{416,16},{385,1},{417,17},{386,2},{418,18},{387,3},{419,19... | collective-permute-start | bytes 9224 | tf_op jit(solution)/shard_map/ppermute | solution.py:272
  34.6 0.7 %collective-permute-start.6 = (f32[2,384]{1,0:T(2,128)S(1)}, f32[2,384]{1,0:T(2,128)S(1)}, u32[]{:S(2)}, u32[]{:S(2)}) collective-permute-start(f32[2,384]{1,0:T(2,128)S(1)} %add.29), channel_id=1, source_target_pairs={{256,0},{257,1},{258,2},{259,3},{260,4},{261,5},{262,6},{263,7},{2... | collective-permute-start | bytes 9224 | tf_op jit(solution)/shard_map/ppermute | solution.py:272
  35.3 2.8 %collective-permute-done.1 = f32[2,384]{1,0:T(2,128)S(1)} collective-permute-done((f32[2,384]{1,0:T(2,128)S(1)}, f32[2,384]{1,0:T(2,128)S(1)}, u32[]{:S(2)}, u32[]{:S(2)}) %collective-permute-start.1) | collective-permute-done | bytes 3104 | tf_op jit(solution)/shard_map/ppermute | solution.py:272
  38.1 1.3 %collective-permute-start.5 = (f32[2,384]{1,0:T(2,128)S(1)}, f32[2,384]{1,0:T(2,128)S(1)}, u32[]{:S(2)}, u32[]{:S(2)}) collective-permute-start(f32[2,384]{1,0:T(2,128)S(1)} %add.29), channel_id=1, source_target_pairs={{448,0},{480,16},{449,1},{481,17},{450,2},{482,18},{451,3},{483,19... | collective-permute-start | bytes 9224 | tf_op jit(solution)/shard_map/ppermute | solution.py:272
  39.4 0.7 %select_add_fusion = f32[8,2,384]{2,1,0:T(2,128)} fusion(pred[2]{0:T(512)(128)(4,1)S(1)} %iota_compare_fusion.1, f32[2,384]{1,0:T(2,128)S(1)} %collective-permute-done.1, f32[2,384]{1,0:T(2,128)S(1)} %get-tuple-element.13), kind=kLoop, calls=%fused_computation.1 | loop fusion | flops 12288 | bytes 30722 | tf_op jit(solution)/shard_map/add | solution.py:286
  40.1 4.2 %all-to-all-start.1 = ((f32[8,2,384]{2,1,0:T(2,128)}), f32[8,2,384]{2,1,0:T(2,128)S(1)}, u32[]{:S(2)}, u32[]{:S(2)}) async-start(f32[8,2,384]{2,1,0:T(2,128)} %select_add_fusion), calls=%async_computation.1 | async-start | bytes 49152 | tf_op jit(solution)/shard_map/all_to_all | solution.py:288
  44.3 0.5 collective-permute-done.5
  44.8 0.9 %collective-permute-done.4 = f32[2,384]{1,0:T(2,128)S(1)} collective-permute-done((f32[2,384]{1,0:T(2,128)S(1)}, f32[2,384]{1,0:T(2,128)S(1)}, u32[]{:S(2)}, u32[]{:S(2)}) %collective-permute-start.4) | collective-permute-done | bytes 3104 | tf_op jit(solution)/shard_map/ppermute | solution.py:272
  45.6 0.0 collective-permute-done.2
  45.6 2.3 %collective-permute-start.7 = (f32[2,384]{1,0:T(2,128)S(1)}, f32[2,384]{1,0:T(2,128)S(1)}, u32[]{:S(2)}, u32[]{:S(2)}) collective-permute-start(f32[2,384]{1,0:T(2,128)S(1)} %add_add_fusion), channel_id=1, source_target_pairs={{16,0},{17,1},{18,2},{19,3},{20,4},{21,5},{22,6},{23,7},{24,8},{25... | collective-permute-start | bytes 9224 | tf_op jit(solution)/shard_map/ppermute | solution.py:272
  47.9 1.3 %shard_map.79 = (f32[286,128]{1,0:T(8,128)}, f32[26,286]{1,0:T(8,128)S(1)}) custom-call(f32[16,72,128]{2,1,0:T(8,128)S(1)} %all-to-all-done.got_ref, s32[1,512]{1,0:T(1,128)S(1)} %get-tuple-element.17.rank_ref, f32[80,384]{1,0:T(8,128)S(1)} %get-tuple-element.18.level_ref, s32[4,128]{1,0:T(4,128)S(1)} %get-tuple-element.19.span_ref), custom_call_target="tpu_custom_call" | custom-call | tf_op jit(solution)/shard_map/pallas_call | solution.py:302
  49.2 0.0 all-to-all-done.1
  49.3 0.7 %select_multiply_fusion = f32[26,286]{1,0:T(8,128)} fusion(f32[26,286]{1,0:T(8,128)S(1)} %get-tuple-element.21, f32[286]{0:T(512)S(1)} %get-tuple-element.25, f32[286]{0:T(512)S(1)} %get-tuple-element.24, pred[26]{0:T(512)(128)(4,1)S(1)} %get-tuple-element.26, pred[26]{0:T(512)(128)(4,1)S(1)} %get-tuple-element.27), kind=kLoop, calls=%fused_computation | loop fusion | flops 22308 | bytes 61828 | tf_op jit(solution)/shard_map/mul | solution.py:356
  (12 shorter events, 0.1 us)
Async XLA Ops:
  4.4 17.4 %copy-start = (bf16[256,384]{1,0:T(8,128)(2,1)S(1)}, bf16[256,384]{1,0:T(8,128)(2,1)}, u32[]{:S(2)}) copy-start(bf16[256,384]{1,0:T(8,128)(2,1)} %constant.23.clone.shift_ref) | copy-start | bytes 589828
  4.4 17.4 %all-to-all-start = ((f32[16,72,128]{2,1,0:T(8,128)}), f32[16,72,128]{2,1,0:T(8,128)S(1)}, u32[]{:S(2)}, u32[]{:S(2)}) async-start(f32[16,72,128]{2,1,0:T(8,128)} %shard_map.77), calls=%async_computation | async-start | bytes 1179648 | tf_op jit(solution)/shard_map/all_to_all | solution.py:340
  12.1 9.7 %copy-start.1 = (f32[8,384]{1,0:T(8,128)S(1)}, f32[8,384]{1,0:T(8,128)}, u32[]{:S(2)}) copy-start(f32[8,384]{1,0:T(8,128)} %constant.24.clone.signs_ref) | copy-start | bytes 36868
  23.8 6.9 %collective-permute-start = (f32[2,384]{1,0:T(2,128)S(1)}, f32[2,384]{1,0:T(2,128)S(1)}, u32[]{:S(2)}, u32[]{:S(2)}) collective-permute-start(f32[2,384]{1,0:T(2,128)S(1)} %get-tuple-element.13), channel_id=1, source_target_pairs={{16,0},{48,32},{80,64},{112,96},{144,128},{176,160},{208,192},{240... | collective-permute-start | bytes 9224 | tf_op jit(solution)/shard_map/ppermute | solution.py:272
  29.4 8.7 %collective-permute-start.1 = (f32[2,384]{1,0:T(2,128)S(1)}, f32[2,384]{1,0:T(2,128)S(1)}, u32[]{:S(2)}, u32[]{:S(2)}) collective-permute-start(f32[2,384]{1,0:T(2,128)S(1)} %get-tuple-element.13), channel_id=1, source_target_pairs={{128,0},{144,16},{160,32},{176,48},{192,64},{208,80},{129,1},{145,... | collective-permute-start | bytes 9224 | tf_op jit(solution)/shard_map/ppermute | solution.py:272
  30.7 14.9 %collective-permute-start.4 = (f32[2,384]{1,0:T(2,128)S(1)}, f32[2,384]{1,0:T(2,128)S(1)}, u32[]{:S(2)}, u32[]{:S(2)}) collective-permute-start(f32[2,384]{1,0:T(2,128)S(1)} %add.29), channel_id=1, source_target_pairs={{288,16},{320,0},{289,17},{321,1},{290,18},{322,2},{291,19},{323,3... | collective-permute-start | bytes 9224 | tf_op jit(solution)/shard_map/ppermute | solution.py:272
  32.0 13.6 %collective-permute-start.2 = (f32[2,384]{1,0:T(2,128)S(1)}, f32[2,384]{1,0:T(2,128)S(1)}, u32[]{:S(2)}, u32[]{:S(2)}) collective-permute-start(f32[2,384]{1,0:T(2,128)S(1)} %add.29), channel_id=1, source_target_pairs={{224,0},{352,16},{225,1},{353,17},{226,2},{354,18},{227,3},{355,19... | collective-permute-start | bytes 9224 | tf_op jit(solution)/shard_map/ppermute | solution.py:272
  33.3 12.3 %collective-permute-start.3 = (f32[2,384]{1,0:T(2,128)S(1)}, f32[2,384]{1,0:T(2,128)S(1)}, u32[]{:S(2)}, u32[]{:S(2)}) collective-permute-start(f32[2,384]{1,0:T(2,128)S(1)} %add.29), channel_id=1, source_target_pairs={{384,0},{416,16},{385,1},{417,17},{386,2},{418,18},{387,3},{419,19... | collective-permute-start | bytes 9224 | tf_op jit(solution)/shard_map/ppermute | solution.py:272
  34.6 14.6 %collective-permute-start.6 = (f32[2,384]{1,0:T(2,128)S(1)}, f32[2,384]{1,0:T(2,128)S(1)}, u32[]{:S(2)}, u32[]{:S(2)}) collective-permute-start(f32[2,384]{1,0:T(2,128)S(1)} %add.29), channel_id=1, source_target_pairs={{256,0},{257,1},{258,2},{259,3},{260,4},{261,5},{262,6},{263,7},{2... | collective-permute-start | bytes 9224 | tf_op jit(solution)/shard_map/ppermute | solution.py:272
  38.1 6.6 %collective-permute-start.5 = (f32[2,384]{1,0:T(2,128)S(1)}, f32[2,384]{1,0:T(2,128)S(1)}, u32[]{:S(2)}, u32[]{:S(2)}) collective-permute-start(f32[2,384]{1,0:T(2,128)S(1)} %add.29), channel_id=1, source_target_pairs={{448,0},{480,16},{449,1},{481,17},{450,2},{482,18},{451,3},{483,19... | collective-permute-start | bytes 9224 | tf_op jit(solution)/shard_map/ppermute | solution.py:272
  40.1 9.1 %all-to-all-start.1 = ((f32[8,2,384]{2,1,0:T(2,128)}), f32[8,2,384]{2,1,0:T(2,128)S(1)}, u32[]{:S(2)}, u32[]{:S(2)}) async-start(f32[8,2,384]{2,1,0:T(2,128)} %select_add_fusion), calls=%async_computation.1 | async-start | bytes 49152 | tf_op jit(solution)/shard_map/all_to_all | solution.py:288
  45.6 3.6 %collective-permute-start.7 = (f32[2,384]{1,0:T(2,128)S(1)}, f32[2,384]{1,0:T(2,128)S(1)}, u32[]{:S(2)}, u32[]{:S(2)}) collective-permute-start(f32[2,384]{1,0:T(2,128)S(1)} %add_add_fusion), channel_id=1, source_target_pairs={{16,0},{17,1},{18,2},{19,3},{20,4},{21,5},{22,6},{23,7},{24,8},{25... | collective-permute-start | bytes 9224 | tf_op jit(solution)/shard_map/ppermute | solution.py:272
